TPU v7x, 32 devices: a whole 2x2x4 slice. The times are simulated.
32 devices in a mesh: grp: 4 (over y, core), mem: 8 (over z, x).
Axes of the slice: x: 2, y: 2, z: 4, core: 2. Of those that a mesh axis runs over, the one named last changes fastest.
Arguments:
- amplitudes: bfloat16 [4, 8, 384, 384], P('grp', 'mem'), may hold values from -6 to 6
- integrals: bfloat16 [4, 8, 384, 384], P('grp', 'mem'), may hold values from -0.3125 to 0.3125
- task_list: int32 [4, 512, 3], P('grp'), may hold values from 0 to 7
- task_counts: int32 [4, 8], P('grp'), may hold values from 1 to 64, 256 in all within a row
- owner_map: int32 [8], replicated, may hold values from 0 to 7, each once
Outputs:
- cycle: bfloat16 [4, 8, 384, 384], P('grp', 'mem')
Inputs may be any that keep to these rules, and one draw needn't show every extreme that they name: `task_list`: rows 64 * e to 64 * (e + 1) - 1 of a group are executor e's task slots; every id is a tile id. `task_counts`: the counts of a group sum to 256. `owner_map`: A permutation of the tile ids.
All inputs are finite; a program needn't handle non-finite values.
Results may differ from a plain program's by a relative error of at most 0.014.
Values may be sent and summed in bfloat16 or wider, within the bound.
A program may use at most 192 MiB of HBM per device.

v0:
```python
import math

import jax
import jax.numpy as jnp
from jax import lax
from jax.sharding import PartitionSpec as P

TASK_DEV = 64


def block_products(got_mixed, got_int, picked, living):
    left_tile = jnp.take(got_mixed, picked[:, 1], axis=0)
    right_tile = jnp.take(got_int, picked[:, 2], axis=0)
    product = jnp.einsum("kxy,kyz->kxz", left_tile, right_tile, preferred_element_type=jnp.float32)
    return jnp.where(living[:, None, None], product, jnp.float32(0.0))


def add_targets(running, targets, living, product):
    safe_targets = jnp.where(living, targets, 0)
    return running.at[safe_targets].add(product)


def local(amplitudes, integrals, task_list, task_counts, owner_map):
    tile_order = amplitudes.shape[-1]
    members = lax.axis_size("mem")
    device = lax.axis_index("mem")
    slot_count = TASK_DEV
    own_amp = amplitudes[0, 0]
    swapped = lax.all_to_all(own_amp, "grp", split_axis=0, concat_axis=0, tiled=True)
    mixed_tile = (2.0 * own_amp.astype(jnp.float32) - swapped.astype(jnp.float32)).astype(
        jnp.bfloat16
    )
    own_int = integrals[0, 0]
    holders = jnp.take(owner_map, task_list[0], axis=0)
    live_all = jnp.arange(slot_count, dtype=jnp.int32)[None, :] < task_counts[0][:, None]
    got_mixed, got_int = (
        lax.all_gather(mixed_tile[None], "mem", axis=0, tiled=True),
        lax.all_gather(own_int[None], "mem", axis=0, tiled=True),
    )
    flat_live = live_all.reshape(-1)
    mine = flat_live & (holders[:, 0] == device)
    order = jnp.argsort(jnp.where(mine, 0, 1).astype(jnp.int32), stable=True)
    total_mine = jnp.sum(mine.astype(jnp.int32))
    block_size = math.gcd(members * slot_count, 16)
    block_count = (total_mine + block_size - 1) // block_size
    slot_index = jnp.arange(block_size, dtype=jnp.int32)

    def owner_step(state):
        turn, per_exec = state
        first = turn * block_size
        chosen = lax.dynamic_slice_in_dim(order, first, block_size, 0)
        picked = jnp.take(holders, chosen, axis=0)
        living = slot_index + first < total_mine
        product = block_products(got_mixed, got_int, picked, living)
        return (turn + 1, add_targets(per_exec, chosen // slot_count, living, product))

    start_exec = jnp.zeros((members, tile_order, tile_order), jnp.float32)
    _, per_exec = lax.while_loop(
        lambda state: state[0] < block_count, owner_step, (jnp.int32(0), start_exec)
    )
    summed = jnp.sum(per_exec.astype(jnp.bfloat16), axis=0, dtype=jnp.float32)
    return summed.astype(jnp.bfloat16)[None, None]


def solution(mesh):
    placed = (
        P("grp", "mem", None, None),
        P("grp", "mem", None, None),
        P("grp", None, None),
        P("grp", None),
        P(),
    )
    return jax.shard_map(
        local, mesh=mesh, in_specs=placed, out_specs=P("grp", "mem", None, None), check_vma=False
    )
```

profile of v0, /device:TPU:2, one launch (start us, length us, event | category | flops | bytes accessed | tf_op | source)
XLA Modules:
  0.0 243.5 jit_solution(1171598872209966630)
XLA Ops:
  6.5 0.7 all-gather.6.cloned.1.call-update
  7.3 9.8 %all_to_all.9 = bf16[4,96,384]{2,1,0:T(8,128)(2,1)S(1)} all-to-all(bf16[4,96,384]{2,1,0:T(8,128)(2,1)} %bitcast.30), channel_id=1, replica_groups=mesh['grp'=4,'mem'=8] {'grp'}, dimensions={0} | all-to-all | bytes 589824 | tf_op jit(solution)/shard_map/all_to_all | solution.py:29
  17.1 1.8 fusion.14
  18.9 0.7 iota_compare_fusion
  19.8 1.6 fusion.18
  21.5 5.6 %fusion.15 = s32[512,3]{0,1:T(4,128)S(1)} fusion(s32[512,3,1]{0,2,1:T(1,128)} %bitcast.32, s32[1,512,3]{1,0,2:T(1,128)} %param.11, s32[]{:T(128)} %bitcast.4, s32[]{:T(128)} %bitcast.5, s32[]{:T(128)} %bitcast.6, s32[]{:T(128)} %bitcast.7, s32[]{:T(128)} %bitcast.8, s32[]{:T(128)} %bitcast.10, s32[]{:T(128)} %bitcast.9, s32[]{:T(128)} %bitcast.3), kind=kLoop, calls=%fused_computation.38 | loop fusion | flops 36864 | bytes 18464 | tf_op jit(solution)/shard_map/jit(_take)/select_n | solution.py:34
  28.6 3.8 %sort.17 = (s32[512]{0:T(512)}, s32[512]{0:T(512)S(1)}) sort(s32[512]{0:T(512)S(1)} %and_select_fusion.1, s32[512]{0:T(512)S(1)} %iota.14), dimensions={0}, to_apply=%region_1.2 | sort | flops 4608 | bytes 8192 | tf_op jit(solution)/shard_map/jit(argsort)/sort | solution.py:42
  32.4 29.9 %all-gather.6.cloned.1.call-done = bf16[8,1,384,384]{3,2,1,0:T(8,128)(2,1)} async-done(((bf16[1,1,384,384]{3,2,1,0:T(8,128)(2,1)}), bf16[8,1,384,384]{3,2,1,0:T(8,128)(2,1)}) %all-gather.6.cloned.1.call-update) | async-done | bytes 2359312 | tf_op jit(solution)/shard_map/all_gather | solution.py:38
  62.3 52.8 %all-gather.4.cloned.1.call-done = bf16[8,384,384]{2,1,0:T(8,128)(2,1)} async-done(((bf16[1,384,384]{2,1,0:T(8,128)(2,1)}), bf16[8,384,384]{2,1,0:T(8,128)(2,1)}) %all-gather.4.cloned.1.call-update) | async-done | bytes 2359312 | tf_op jit(solution)/shard_map/all_gather | solution.py:37
  115.1 2.6 %broadcast_in_dim.80 = f32[8,384,384]{2,1,0:T(8,128)} broadcast(f32[]{:T(128)} %constant.122.clone.1), dimensions={} | broadcast | bytes 4718596 | tf_op jit(solution)/shard_map/broadcast_in_dim | solution.py:57
  117.7 115.6 %while.13 = (s32[]{:T(128)}, f32[8,384,384]{2,1,0:T(8,128)}, s32[]{:T(128)}, s32[]{:T(128)}, s32[512]{0:T(512)S(1)}, /*index=5*/s32[512,3]{1,0:T(8,128)S(1)}, bf...) while((s32[]{:T(128)}, f32[8,384,384]{2,1,0:T(8,128)}, ...), condition=%wide.region_4.6_spmd.clone, body=%wide.region_2.5_spmd.clone.sunk | while | flops 1821380352 | bytes 66074992 | solution.py:58
  119.4 5.0 %gather_fusion.2 = bf16[16,384,384]{2,1,0:T(8,128)(2,1)} fusion(bf16[8,384,384]{2,1,0:T(8,128)(2,1)} %get-tuple-element.303, s32[1024]{0:T(1024)S(1)} %pad_clamp_fusion.8), kind=kCustom, calls=%fused_computation.clone.clone.1 | custom fusion | bytes 9437248 | tf_op jit(solution)/shard_map/while/body/jit(_take)/gather | solution.py:12
  124.4 3.3 %gather_fusion.1 = bf16[16,384,384]{2,1,0:T(8,128)(2,1)} fusion(bf16[8,384,384]{2,1,0:T(8,128)(2,1)S(1)} %get-tuple-element.304, s32[1024]{0:T(1024)S(1)} %pad_clamp_fusion.7), kind=kCustom, calls=%fused_computation.1.clone.clone.1 | custom fusion | bytes 9437248 | tf_op jit(solution)/shard_map/while/body/jit(_take)/gather | solution.py:13
  127.7 10.5 %broadcast_select_fusion.5 = f32[16,384,384]{2,1,0:T(8,128)} fusion(pred[16]{0:T(512)(128)(4,1)S(1)} %get-tuple-element.264, bf16[16,384,384]{2,1,0:T(8,128)(2,1)} %gather_fusion.1, pred[16]{0:T(512)(128)(4,1)S(1)} %get-tuple-element.270, bf16[16,384,384]{2,1,0:T(8,128)(2,1)} %gather_fusion.2, pred[16]{0:T(512)(128)(4,1)S(1)} %get-tuple-element.272), kind=kOutput, calls=%fused_computation.8.clone.1 | convolution fusion | flops 1819017216 | bytes 18874416 | tf_op jit(solution)/shard_map/while/body/kxy,kyz->kxz/dot_general | solution.py:14
  138.3 18.1 %scatter_fusion = f32[8,384,384]{2,1,0:T(8,128)} fusion(f32[8,384,384]{2,1,0:T(8,128)} %get-tuple-element.286, s32[16]{0:T(128)S(1)} %get-tuple-element.263, f32[16,384,384]{2,1,0:T(8,128)} %broadcast_select_fusion.5), kind=kCustom, calls=%fused_computation.3.clone.clone.1 | custom fusion | flops 2359296 | bytes 28311616 | tf_op jit(solution)/shard_map/while/body/scatter-add | solution.py:20
  158.0 5.0 %gather_fusion.2 = bf16[16,384,384]{2,1,0:T(8,128)(2,1)} fusion(bf16[8,384,384]{2,1,0:T(8,128)(2,1)} %get-tuple-element.303, s32[1024]{0:T(1024)S(1)} %pad_clamp_fusion.8), kind=kCustom, calls=%fused_computation.clone.clone.1 | custom fusion | bytes 9437248 | tf_op jit(solution)/shard_map/while/body/jit(_take)/gather | solution.py:12
  163.1 3.3 %gather_fusion.1 = bf16[16,384,384]{2,1,0:T(8,128)(2,1)} fusion(bf16[8,384,384]{2,1,0:T(8,128)(2,1)S(1)} %get-tuple-element.304, s32[1024]{0:T(1024)S(1)} %pad_clamp_fusion.7), kind=kCustom, calls=%fused_computation.1.clone.clone.1 | custom fusion | bytes 9437248 | tf_op jit(solution)/shard_map/while/body/jit(_take)/gather | solution.py:13
  166.4 10.5 %broadcast_select_fusion.5 = f32[16,384,384]{2,1,0:T(8,128)} fusion(pred[16]{0:T(512)(128)(4,1)S(1)} %get-tuple-element.264, bf16[16,384,384]{2,1,0:T(8,128)(2,1)} %gather_fusion.1, pred[16]{0:T(512)(128)(4,1)S(1)} %get-tuple-element.270, bf16[16,384,384]{2,1,0:T(8,128)(2,1)} %gather_fusion.2, pred[16]{0:T(512)(128)(4,1)S(1)} %get-tuple-element.272), kind=kOutput, calls=%fused_computation.8.clone.1 | convolution fusion | flops 1819017216 | bytes 18874416 | tf_op jit(solution)/shard_map/while/body/kxy,kyz->kxz/dot_general | solution.py:14
  176.9 18.2 %scatter_fusion = f32[8,384,384]{2,1,0:T(8,128)} fusion(f32[8,384,384]{2,1,0:T(8,128)} %get-tuple-element.286, s32[16]{0:T(128)S(1)} %get-tuple-element.263, f32[16,384,384]{2,1,0:T(8,128)} %broadcast_select_fusion.5), kind=kCustom, calls=%fused_computation.3.clone.clone.1 | custom fusion | flops 2359296 | bytes 28311616 | tf_op jit(solution)/shard_map/while/body/scatter-add | solution.py:20
  196.8 5.0 %gather_fusion.2 = bf16[16,384,384]{2,1,0:T(8,128)(2,1)} fusion(bf16[8,384,384]{2,1,0:T(8,128)(2,1)} %get-tuple-element.303, s32[1024]{0:T(1024)S(1)} %pad_clamp_fusion.8), kind=kCustom, calls=%fused_computation.clone.clone.1 | custom fusion | bytes 9437248 | tf_op jit(solution)/shard_map/while/body/jit(_take)/gather | solution.py:12
  201.8 3.3 %gather_fusion.1 = bf16[16,384,384]{2,1,0:T(8,128)(2,1)} fusion(bf16[8,384,384]{2,1,0:T(8,128)(2,1)S(1)} %get-tuple-element.304, s32[1024]{0:T(1024)S(1)} %pad_clamp_fusion.7), kind=kCustom, calls=%fused_computation.1.clone.clone.1 | custom fusion | bytes 9437248 | tf_op jit(solution)/shard_map/while/body/jit(_take)/gather | solution.py:13
  205.2 10.5 %broadcast_select_fusion.5 = f32[16,384,384]{2,1,0:T(8,128)} fusion(pred[16]{0:T(512)(128)(4,1)S(1)} %get-tuple-element.264, bf16[16,384,384]{2,1,0:T(8,128)(2,1)} %gather_fusion.1, pred[16]{0:T(512)(128)(4,1)S(1)} %get-tuple-element.270, bf16[16,384,384]{2,1,0:T(8,128)(2,1)} %gather_fusion.2, pred[16]{0:T(512)(128)(4,1)S(1)} %get-tuple-element.272), kind=kOutput, calls=%fused_computation.8.clone.1 | convolution fusion | flops 1819017216 | bytes 18874416 | tf_op jit(solution)/shard_map/while/body/kxy,kyz->kxz/dot_general | solution.py:14
  215.7 17.6 %scatter_fusion = f32[8,384,384]{2,1,0:T(8,128)} fusion(f32[8,384,384]{2,1,0:T(8,128)} %get-tuple-element.286, s32[16]{0:T(128)S(1)} %get-tuple-element.263, f32[16,384,384]{2,1,0:T(8,128)} %broadcast_select_fusion.5), kind=kCustom, calls=%fused_computation.3.clone.clone.1 | custom fusion | flops 2359296 | bytes 28311616 | tf_op jit(solution)/shard_map/while/body/scatter-add | solution.py:20
  233.3 3.4 %convert_reduce_fusion = bf16[384,384]{1,0:T(8,128)(2,1)} fusion(f32[8,384,384]{2,1,0:T(8,128)} %get-tuple-element.125), kind=kLoop, calls=%fused_computation.32 | loop fusion | flops 2211840 | bytes 5013504 | tf_op jit(solution)/shard_map/reduce_sum | solution.py:61
  (42 shorter events, 6.0 us)
Async XLA Ops:
  6.5 55.7 %all-gather.6.cloned.1.call-start = ((), (), s32[]{:S(2)}) async-start(), calls=%async_computation.2 | async-start | bytes 2654208 | tf_op jit(solution)/shard_map/all_gather | solution.py:38
  7.3 107.8 %all-gather.4.cloned.1.call-start = ((), (), s32[]{:S(2)}) async-start(), calls=%async_computation.1 | async-start | bytes 2654208 | tf_op jit(solution)/shard_map/all_gather | solution.py:37
  62.2 55.5 %copy-start = (bf16[8,1,384,384]{3,2,1,0:T(8,128)(2,1)S(1)}, bf16[8,1,384,384]{3,2,1,0:T(8,128)(2,1)}, u32[]{:S(2)}) copy-start(bf16[8,1,384,384]{3,2,1,0:T(8,128)(2,1)} %all-gather.6.cloned.1.call-done) | copy-start | bytes 7077892
Sparse Core Ops, SparseCore 0:
  9.5 52.6 all-gather.5
  64.4 50.6 all-gather.3
where the time goes:
time: 246 us; the launch traced here: 243 us
  waiting for transfers between devices  83.4 us (34%)
  other arithmetic  72.4 us (29%)
  local copies, waits for them, and re-layouts  32 us (13%)
  matrix products  31.6 us (13%)
  between operations  14.1 us (6%)
  blocking collectives  9.82 us (4%)
    scatter-add x3, other arithmetic, add_targets(): return running.at[safe_targets].add(product)  53.8 us
    all_gather x1, waiting for transfers between devices, local(): lax.all_gather(mixed_tile[None], 'mem', axis=0, tiled=True)  52.8 us
    dot_general x3, matrix products, block_products(): jnp.einsum('kxy,kyz->kxz', left_tile, right_tile, preferred_element_type=...  31.6 us
    all_gather x1, waiting for transfers between devices, local(): lax.all_gather(own_int[None], 'mem', axis=0, tiled=True)  29.9 us
    gather x3, local copies, waits for them, and re-layouts, block_products(): left_tile = jnp.take(got_mixed, picked[:, 1], axis=0)  15.1 us
    gather x3, local copies, waits for them, and re-layouts, block_products(): right_tile = jnp.take(got_int, picked[:, 2], axis=0)  10 us
    all_to_all x1, blocking collectives, local(): lax.all_to_all(own_amp, 'grp', split_axis=0, concat_axis=0, tiled=True)  9.82 us
    select_n x1, other arithmetic, local(): holders = jnp.take(owner_map, task_list[0], axis=0)  5.62 us
  transfers between devices with their start and end apart: 2, of which 2 were waited for; matrix products, arithmetic and copies ran while one was open for 6% of the time, Pallas kernels for 0%

commit v1 on v0

--- a/solution.py
+++ b/solution.py
@@ -1,8 +1,11 @@
+import functools
 import math
 
 import jax
 import jax.numpy as jnp
 from jax import lax
+from jax.experimental import pallas as pl
+from jax.experimental.pallas import tpu as pltpu
 from jax.sharding import PartitionSpec as P
 
 TASK_DEV = 64
@@ -62,6 +65,253 @@
     return summed.astype(jnp.bfloat16)[None, None]
 
 
+MESH = pl.DeviceIdType.MESH
+STEP = 128
+
+
+def remote(src, dst, send_sem, recv_sem, **place):
+    return pltpu.make_async_remote_copy(
+        src_ref=src, dst_ref=dst, send_sem=send_sem, recv_sem=recv_sem,
+        device_id=place, device_id_type=MESH,
+    )
+
+
+def count_tasks(members, tasks, counts, owner):
+    total = tasks.shape[-1]
+    slots = total // members
+    ids = [tasks[field] for field in range(3)]
+    rows = [jnp.zeros((1, total), jnp.int32) for _ in range(3)]
+    for tile_id in range(members):
+        row = owner[tile_id]
+        rows = [jnp.where(ids[f] == tile_id, row, rows[f]) for f in range(3)]
+    place = lax.broadcasted_iota(jnp.int32, (1, total), 1)
+    live = jnp.zeros((1, total), jnp.int32)
+    for executor in range(members):
+        offset = place - executor * slots
+        inside = (offset >= 0) & (offset < jnp.minimum(counts[0, executor], slots))
+        live = jnp.where(inside, 1, live)
+    target = jnp.where(live == 1, rows[0], -1)
+    pair = rows[1] * members + rows[2]
+    hot_target = lax.broadcasted_iota(jnp.int32, (members, total), 0) == target
+    hot_pair = lax.broadcasted_iota(jnp.int32, (members * members, total), 0) == pair
+    return lax.dot_general(
+        jnp.where(hot_target, 1.0, 0.0).astype(jnp.bfloat16),
+        jnp.where(hot_pair, 1.0, 0.0).astype(jnp.bfloat16),
+        (((1,), (1,)), ((), ())),
+        preferred_element_type=jnp.float32,
+    )
+
+
+def cycle_kernel(
+    groups, members,
+    amp, integ, tasks, counts, owner, out,
+    swap, halves, mixed_t, got_t, weighed, parts, landed, table, numbers,
+    swap_ss, swap_rs, int_ss, int_rs, mix_ss, mix_rs, part_ss, part_rs, table_sem,
+):
+    grp, mem = lax.axis_index("grp"), lax.axis_index("mem")
+    tile = amp.shape[-1]
+    half, block, rounds = tile // 2, tile // groups, tile // STEP
+    quarter = members // 2
+    first_worker = members // 2 - 2
+    workers = range(first_worker, first_worker + 4)
+    plane, side = lax.div(mem, 2), lax.rem(mem, 2)
+    area = lax.div(mem, quarter)
+    works = (mem >= first_worker) & (mem < first_worker + 4)
+    own_rows = pl.ds(pl.multiple_of(side * half, half), half)
+
+    barrier = pltpu.get_barrier_semaphore()
+    for turn in range(1, groups):
+        pl.semaphore_signal(
+            barrier, inc=1, device_id={"grp": lax.rem(grp + turn, groups)}, device_id_type=MESH
+        )
+    for turn in range(1, members):
+        pl.semaphore_signal(
+            barrier, inc=1, device_id={"mem": lax.rem(mem + turn, members)}, device_id_type=MESH
+        )
+    pl.semaphore_wait(barrier, groups + members - 2)
+
+    def swap_copy(peer):
+        return remote(
+            amp.at[0, 0, pl.ds(pl.multiple_of(peer * block, block), block)],
+            swap.at[grp], swap_ss.at[peer], swap_rs.at[grp], grp=peer,
+        )
+
+    def int_copy(index, worker):
+        return remote(
+            integ.at[0, 0, pl.ds((worker % 2) * half, half)],
+            halves.at[mem], int_ss.at[index], int_rs.at[mem], mem=worker,
+        )
+
+    def mix_copy(turn, index, worker):
+        return remote(
+            mixed_t.at[turn, pl.ds((worker % 2) * half, half)],
+            got_t.at[turn, mem], mix_ss.at[turn, index], mix_rs.at[turn, mem], mem=worker,
+        )
+
+    def part_copy(turn, index, target):
+        rows = pl.ds(turn * STEP, STEP)
+        return remote(
+            parts.at[index, rows], landed.at[side, rows],
+            part_ss.at[turn, index], part_rs.at[turn, side], mem=target,
+        )
+
+    for turn in range(1, groups):
+        swap_copy(lax.rem(grp + turn, groups)).start()
+    for index, worker in enumerate(workers):
+        @pl.when(mem != worker)
+        def _():
+            int_copy(index, worker).start()
+
+    own_block = pl.ds(pl.multiple_of(grp * block, block), block)
+    swap[grp] = amp[0, 0, own_block]
+
+    @pl.when(works)
+    def _():
+        halves[mem] = integ[0, 0, own_rows]
+        table[...] = count_tasks(members, tasks, counts, owner)
+        to_scalar = pltpu.make_async_copy(table, numbers, table_sem)
+        to_scalar.start()
+        to_scalar.wait()
+
+    for turn in range(1, groups):
+        peer = lax.rem(grp + turn, groups)
+        remote(
+            swap.at[peer], swap.at[peer], swap_ss.at[peer], swap_rs.at[peer], grp=peer
+        ).wait_recv()
+    for turn in range(rounds):
+        rows = pl.ds(turn * STEP, STEP)
+        swapped = swap[...].reshape(tile, tile)[turn * STEP : (turn + 1) * STEP]
+        mixed = (
+            2.0 * amp[0, 0, rows].astype(jnp.float32) - swapped.astype(jnp.float32)
+        )
+        mixed_t[turn] = mixed.T.astype(jnp.bfloat16)
+        for index, worker in enumerate(workers):
+            @pl.when(mem != worker)
+            def _():
+                mix_copy(turn, index, worker).start()
+
+        @pl.when(works)
+        def _():
+            got_t[turn, mem] = mixed_t[turn, own_rows]
+
+    @pl.when(works)
+    def _():
+        for source in range(members):
+            @pl.when(mem != source)
+            def _():
+                remote(
+                    halves.at[source], halves.at[source],
+                    int_ss.at[0], int_rs.at[source], mem=source,
+                ).wait_recv()
+
+        def weigh(index, carry):
+            rows = pl.ds(pl.multiple_of(index * 16, 16), 16)
+            read = [halves[b, rows].astype(jnp.float32) for b in range(members)]
+            for a in range(members):
+                for q in range(quarter):
+                    total = jnp.zeros((16, tile), jnp.float32)
+                    for b in range(members):
+                        total += numbers[area * quarter + q, a * members + b] * read[b]
+                    weighed[q, a, rows] = total.astype(jnp.bfloat16)
+            return carry
+
+        lax.fori_loop(0, half // 16, weigh, 0)
+
+        for turn in range(rounds):
+            rows = pl.ds(turn * STEP, STEP)
+            for source in range(members):
+                @pl.when(mem != source)
+                def _():
+                    remote(
+                        got_t.at[turn, source], got_t.at[turn, source],
+                        mix_ss.at[turn, 0], mix_rs.at[turn, source], mem=source,
+                    ).wait_recv()
+            left = got_t[turn].reshape(members * half, STEP).T
+            for q in range(quarter):
+                target = area * quarter + q
+                parts[q, rows] = jnp.dot(
+                    left, weighed[q].reshape(members * half, tile),
+                    preferred_element_type=jnp.float32,
+                ).astype(jnp.bfloat16)
+
+                @pl.when(mem != target)
+                def _():
+                    part_copy(turn, q, target).start()
+
+                @pl.when(mem == target)
+                def _():
+                    landed[side, rows] = parts[q, rows]
+
+    for turn in range(rounds):
+        rows = pl.ds(turn * STEP, STEP)
+        for sender_side in range(2):
+            sender = lax.min(lax.max(plane, quarter // 2 - 1), quarter // 2) * 2 + sender_side
+
+            @pl.when(mem != sender)
+            def _():
+                remote(
+                    landed.at[sender_side, rows], landed.at[sender_side, rows],
+                    part_ss.at[turn, 0], part_rs.at[turn, sender_side], mem=sender,
+                ).wait_recv()
+        out[0, 0, rows] = (
+            landed[0, rows].astype(jnp.float32) + landed[1, rows].astype(jnp.float32)
+        ).astype(jnp.bfloat16)
+
+    for turn in range(1, groups):
+        swap_copy(lax.rem(grp + turn, groups)).wait_send()
+    for index, worker in enumerate(workers):
+        @pl.when(mem != worker)
+        def _():
+            int_copy(index, worker).wait_send()
+            for turn in range(rounds):
+                mix_copy(turn, index, worker).wait_send()
+
+    @pl.when(works)
+    def _():
+        for q in range(quarter):
+            target = area * quarter + q
+
+            @pl.when(mem != target)
+            def _():
+                for turn in range(rounds):
+                    part_copy(turn, q, target).wait_send()
+
+
+def local_workers(amplitudes, integrals, task_list, task_counts, owner_map):
+    groups, members = lax.axis_size("grp"), lax.axis_size("mem")
+    tile = amplitudes.shape[-1]
+    half, rounds, quarter = tile // 2, tile // STEP, members // 2
+    vmem = pl.BlockSpec(memory_space=pltpu.VMEM)
+    smem = pl.BlockSpec(memory_space=pltpu.SMEM)
+    dma = pltpu.SemaphoreType.DMA
+    bf16 = jnp.bfloat16
+    return pl.pallas_call(
+        functools.partial(cycle_kernel, groups, members),
+        out_shape=jax.ShapeDtypeStruct(amplitudes.shape, bf16),
+        in_specs=[vmem, vmem, vmem, smem, smem],
+        out_specs=vmem,
+        scratch_shapes=[
+            pltpu.VMEM((groups, tile // groups, tile), bf16),
+            pltpu.VMEM((members, half, tile), bf16),
+            pltpu.VMEM((rounds, tile, STEP), bf16),
+            pltpu.VMEM((rounds, members, half, STEP), bf16),
+            pltpu.VMEM((quarter, members, half, tile), bf16),
+            pltpu.VMEM((quarter, tile, tile), bf16),
+            pltpu.VMEM((2, tile, tile), bf16),
+            pltpu.VMEM((members, members * members), jnp.float32),
+            pltpu.SMEM((members, members * members), jnp.float32),
+            dma((groups,)), dma((groups,)),
+            dma((4,)), dma((members,)),
+            dma((rounds, 4)), dma((rounds, members)),
+            dma((rounds, quarter)), dma((rounds, 2)),
+            dma,
+        ],
+        compiler_params=pltpu.CompilerParams(
+            collective_id=0, has_side_effects=True, vmem_limit_bytes=40 * 1024 * 1024
+        ),
+    )(amplitudes, integrals, jnp.transpose(task_list, (2, 0, 1)), task_counts, owner_map)
+
+
 def solution(mesh):
     placed = (
         P("grp", "mem", None, None),
@@ -70,6 +320,7 @@
         P("grp", None),
         P(),
     )
+    body = local_workers if mesh.shape["mem"] == 2 * 4 else local
     return jax.shard_map(
-        local, mesh=mesh, in_specs=placed, out_specs=P("grp", "mem", None, None), check_vma=False
-    )
+        body, mesh=mesh, in_specs=placed, out_specs=P("grp", "mem", None, None), check_vma=False
+    )

time: 246 us -> 46.1 us (0.19)
  the two profiles are of different devices: /device:TPU:2 before, /device:TPU:0 now
where the time goes in v1:
time: 46.1 us; the launch traced here: 45.9 us
  Pallas kernels  41.9 us (91%)
  local copies, waits for them, and re-layouts  4 us (9%)
    pallas_call x1, Pallas kernels, local_workers(): pl.pallas_call(functools.partial(cycle_kernel, groups, members), out_shap...  41.9 us
    unnamed x11, local copies, waits for them, and re-layouts  4 us

profile of v1, /device:TPU:0, one launch (start us, length us, event | category | flops | bytes accessed | tf_op | source)
XLA Modules:
  0.0 45.9 jit_solution(2055549366291040439)
XLA Ops:
  0.0 0.0 copy-start.4
  0.0 0.0 copy-start.3
  0.0 0.7 %copy-done.4 = s32[8]{0:T(128)S(1)} copy-done((s32[8]{0:T(128)S(1)}, s32[8]{0:T(128)}, u32[]{:S(2)}) %copy-start.4) | copy-done | bytes 56
  0.7 0.0 copy-done.3
  0.7 0.0 copy-start
  0.7 1.0 %copy-done = bf16[1,1,384,384]{3,2,1,0:T(8,128)(2,1)S(1)} copy-done((bf16[1,1,384,384]{3,2,1,0:T(8,128)(2,1)S(1)}, bf16[1,1,384,384]{3,2,1,0:T(8,128)(2,1)}, u32[]{:S(2)}) %copy-start) | copy-done | bytes 294936
  1.6 0.0 copy-start.1
  1.6 1.0 %copy-done.1 = bf16[1,1,384,384]{3,2,1,0:T(8,128)(2,1)S(1)} copy-done((bf16[1,1,384,384]{3,2,1,0:T(8,128)(2,1)S(1)}, bf16[1,1,384,384]{3,2,1,0:T(8,128)(2,1)}, u32[]{:S(2)}) %copy-start.1) | copy-done | bytes 294936
  2.6 0.0 copy-start.2
  2.6 0.7 %copy-done.2 = s32[1,512,3]{1,0,2:T(1,128)S(1)} copy-done((s32[1,512,3]{1,0,2:T(1,128)S(1)}, s32[1,512,3]{1,0,2:T(1,128)}, u32[]{:S(2)}) %copy-start.2) | copy-done | bytes 6168
  3.3 41.9 %shard_map.55 = bf16[1,1,384,384]{3,2,1,0:T(8,128)(2,1)S(1)} custom-call(bf16[1,1,384,384]{3,2,1,0:T(8,128)(2,1)S(1)} %copy-done, bf16[1,1,384,384]{3,2,1,0:T(8,128)(2,1)S(1)} %copy-done.1, s32[3,1,512]{2,1,0:T(1,128)S(1)} %bitcast.1, s32[1,8]{1,0:T(1,128)S(1)} %copy-done.3, s32[8]{0:T(128)S(1)} %copy-done.4), custom_call_target="tpu_custom_call" | custom-call | tf_op jit(solution)/shard_map/pallas_call | solution.py:288
  45.2 0.7 %copy.7 = bf16[1,1,384,384]{3,2,1,0:T(8,128)(2,1)} copy(bf16[1,1,384,384]{3,2,1,0:T(8,128)(2,1)S(1)} %shard_map.55) | data formatting | bytes 589824
Async XLA Ops:
  0.0 0.7 %copy-start.4 = (s32[8]{0:T(128)S(1)}, s32[8]{0:T(128)}, u32[]{:S(2)}) copy-start(s32[8]{0:T(128)} %owner.1) | copy-start | bytes 100
  0.0 0.7 %copy-start.3 = (s32[1,8]{1,0:T(1,128)S(1)}, s32[1,8]{1,0:T(1,128)}, u32[]{:S(2)}) copy-start(s32[1,8]{1,0:T(1,128)} %counts.1) | copy-start | bytes 100
  0.7 1.0 %copy-start = (bf16[1,1,384,384]{3,2,1,0:T(8,128)(2,1)S(1)}, bf16[1,1,384,384]{3,2,1,0:T(8,128)(2,1)}, u32[]{:S(2)}) copy-start(bf16[1,1,384,384]{3,2,1,0:T(8,128)(2,1)} %amp.1) | copy-start | bytes 884740
  1.6 1.0 %copy-start.1 = (bf16[1,1,384,384]{3,2,1,0:T(8,128)(2,1)S(1)}, bf16[1,1,384,384]{3,2,1,0:T(8,128)(2,1)}, u32[]{:S(2)}) copy-start(bf16[1,1,384,384]{3,2,1,0:T(8,128)(2,1)} %integ.1) | copy-start | bytes 884740
  2.6 0.7 %copy-start.2 = (s32[1,512,3]{1,0,2:T(1,128)S(1)}, s32[1,512,3]{1,0,2:T(1,128)}, u32[]{:S(2)}) copy-start(s32[1,512,3]{1,0,2:T(1,128)} %param.7) | copy-start | bytes 18436

commit v2 on v1

--- a/solution.py
+++ b/solution.py
@@ -67,6 +67,8 @@
 
 MESH = pl.DeviceIdType.MESH
 STEP = 128
+BAND = 32
+VMEM_BYTES = 65280 * 1024
 
 
 def remote(src, dst, send_sem, recv_sem, **place):
@@ -76,7 +78,7 @@
     )
 
 
-def count_tasks(members, tasks, counts, owner):
+def spread_counts(members, quarter, area, tasks, counts, owner):
     total = tasks.shape[-1]
     slots = total // members
     ids = [tasks[field] for field in range(3)]
@@ -90,23 +92,28 @@
         offset = place - executor * slots
         inside = (offset >= 0) & (offset < jnp.minimum(counts[0, executor], slots))
         live = jnp.where(inside, 1, live)
-    target = jnp.where(live == 1, rows[0], -1)
-    pair = rows[1] * members + rows[2]
-    hot_target = lax.broadcasted_iota(jnp.int32, (members, total), 0) == target
-    hot_pair = lax.broadcasted_iota(jnp.int32, (members * members, total), 0) == pair
-    return lax.dot_general(
-        jnp.where(hot_target, 1.0, 0.0).astype(jnp.bfloat16),
-        jnp.where(hot_pair, 1.0, 0.0).astype(jnp.bfloat16),
+    key = (rows[0] - area * quarter) * members + rows[1]
+    key = jnp.where(live == 1, key, -1)
+    tall, wide = quarter * members * BAND, members * BAND
+    hot_left = lax.broadcasted_iota(jnp.int32, (tall, total), 0) // BAND == key
+    hot_right = lax.broadcasted_iota(jnp.int32, (wide, total), 0) // BAND == rows[2]
+    spread = lax.dot_general(
+        jnp.where(hot_left, 1.0, 0.0).astype(jnp.bfloat16),
+        jnp.where(hot_right, 1.0, 0.0).astype(jnp.bfloat16),
         (((1,), (1,)), ((), ())),
         preferred_element_type=jnp.float32,
     )
+    down = lax.broadcasted_iota(jnp.int32, (tall, wide), 0) % BAND
+    across = lax.broadcasted_iota(jnp.int32, (tall, wide), 1) % BAND
+    return jnp.where(down == across, spread, 0.0).astype(jnp.bfloat16)
 
 
 def cycle_kernel(
     groups, members,
-    amp, integ, tasks, counts, owner, out,
-    swap, halves, mixed_t, got_t, weighed, parts, landed, table, numbers,
-    swap_ss, swap_rs, int_ss, int_rs, mix_ss, mix_rs, part_ss, part_rs, table_sem,
+    amp_hbm, integ, tasks_hbm, counts_hbm, owner_hbm, out,
+    amp, tasks, counts, owner, result,
+    swap, halves, mixed_t, got_t, weighed, parts, landed, spread,
+    swap_ss, swap_rs, int_ss, int_rs, mix_ss, mix_rs, part_ss, part_rs, local_sem, out_sem,
 ):
     grp, mem = lax.axis_index("grp"), lax.axis_index("mem")
     tile = amp.shape[-1]
@@ -119,6 +126,20 @@
     works = (mem >= first_worker) & (mem < first_worker + 4)
     own_rows = pl.ds(pl.multiple_of(side * half, half), half)
 
+    amp_in = pltpu.make_async_copy(amp_hbm, amp, local_sem.at[0])
+    tasks_in = pltpu.make_async_copy(tasks_hbm, tasks, local_sem.at[1])
+    counts_in = pltpu.make_async_copy(counts_hbm, counts, local_sem.at[2])
+    owner_in = pltpu.make_async_copy(owner_hbm, owner, local_sem.at[3])
+    half_in = pltpu.make_async_copy(integ.at[0, 0, own_rows], halves.at[mem], local_sem.at[4])
+    amp_in.start()
+
+    @pl.when(works)
+    def _():
+        tasks_in.start()
+        counts_in.start()
+        owner_in.start()
+        half_in.start()
+
     barrier = pltpu.get_barrier_semaphore()
     for turn in range(1, groups):
         pl.semaphore_signal(
@@ -132,7 +153,7 @@
 
     def swap_copy(peer):
         return remote(
-            amp.at[0, 0, pl.ds(pl.multiple_of(peer * block, block), block)],
+            amp_hbm.at[0, 0, pl.ds(pl.multiple_of(peer * block, block), block)],
             swap.at[grp], swap_ss.at[peer], swap_rs.at[grp], grp=peer,
         )
 
@@ -154,6 +175,10 @@
             parts.at[index, rows], landed.at[side, rows],
             part_ss.at[turn, index], part_rs.at[turn, side], mem=target,
         )
+
+    def result_copy(turn):
+        rows = pl.ds(turn * STEP, STEP)
+        return pltpu.make_async_copy(result.at[rows], out.at[0, 0, rows], out_sem.at[turn])
 
     for turn in range(1, groups):
         swap_copy(lax.rem(grp + turn, groups)).start()
@@ -162,16 +187,17 @@
         def _():
             int_copy(index, worker).start()
 
+    amp_in.wait()
     own_block = pl.ds(pl.multiple_of(grp * block, block), block)
     swap[grp] = amp[0, 0, own_block]
 
     @pl.when(works)
     def _():
-        halves[mem] = integ[0, 0, own_rows]
-        table[...] = count_tasks(members, tasks, counts, owner)
-        to_scalar = pltpu.make_async_copy(table, numbers, table_sem)
-        to_scalar.start()
-        to_scalar.wait()
+        tasks_in.wait()
+        counts_in.wait()
+        owner_in.wait()
+        half_in.wait()
+        spread[...] = spread_counts(members, quarter, area, tasks, counts, owner)
 
     for turn in range(1, groups):
         peer = lax.rem(grp + turn, groups)
@@ -205,17 +231,15 @@
                 ).wait_recv()
 
         def weigh(index, carry):
-            rows = pl.ds(pl.multiple_of(index * 16, 16), 16)
-            read = [halves[b, rows].astype(jnp.float32) for b in range(members)]
-            for a in range(members):
-                for q in range(quarter):
-                    total = jnp.zeros((16, tile), jnp.float32)
-                    for b in range(members):
-                        total += numbers[area * quarter + q, a * members + b] * read[b]
-                    weighed[q, a, rows] = total.astype(jnp.bfloat16)
+            rows = pl.ds(pl.multiple_of(index * BAND, BAND), BAND)
+            sums = jnp.dot(
+                spread[...], halves[:, rows].reshape(members * BAND, tile),
+                preferred_element_type=jnp.float32,
+            )
+            weighed[:, :, rows] = sums.astype(jnp.bfloat16).reshape(quarter, members, BAND, tile)
             return carry
 
-        lax.fori_loop(0, half // 16, weigh, 0)
+        lax.fori_loop(0, half // BAND, weigh, 0)
 
         for turn in range(rounds):
             rows = pl.ds(turn * STEP, STEP)
@@ -253,9 +277,10 @@
                     landed.at[sender_side, rows], landed.at[sender_side, rows],
                     part_ss.at[turn, 0], part_rs.at[turn, sender_side], mem=sender,
                 ).wait_recv()
-        out[0, 0, rows] = (
+        result[rows] = (
             landed[0, rows].astype(jnp.float32) + landed[1, rows].astype(jnp.float32)
         ).astype(jnp.bfloat16)
+        result_copy(turn).start()
 
     for turn in range(1, groups):
         swap_copy(lax.rem(grp + turn, groups)).wait_send()
@@ -276,21 +301,28 @@
                 for turn in range(rounds):
                     part_copy(turn, q, target).wait_send()
 
+    for turn in range(rounds):
+        result_copy(turn).wait()
+
 
 def local_workers(amplitudes, integrals, task_list, task_counts, owner_map):
     groups, members = lax.axis_size("grp"), lax.axis_size("mem")
     tile = amplitudes.shape[-1]
     half, rounds, quarter = tile // 2, tile // STEP, members // 2
-    vmem = pl.BlockSpec(memory_space=pltpu.VMEM)
-    smem = pl.BlockSpec(memory_space=pltpu.SMEM)
+    hbm = pl.BlockSpec(memory_space=pltpu.HBM)
     dma = pltpu.SemaphoreType.DMA
     bf16 = jnp.bfloat16
     return pl.pallas_call(
         functools.partial(cycle_kernel, groups, members),
         out_shape=jax.ShapeDtypeStruct(amplitudes.shape, bf16),
-        in_specs=[vmem, vmem, vmem, smem, smem],
-        out_specs=vmem,
+        in_specs=[hbm] * 5,
+        out_specs=hbm,
         scratch_shapes=[
+            pltpu.VMEM(amplitudes.shape, bf16),
+            pltpu.VMEM((3, 1, task_list.shape[1]), jnp.int32),
+            pltpu.SMEM(task_counts.shape, jnp.int32),
+            pltpu.SMEM(owner_map.shape, jnp.int32),
+            pltpu.VMEM((tile, tile), bf16),
             pltpu.VMEM((groups, tile // groups, tile), bf16),
             pltpu.VMEM((members, half, tile), bf16),
             pltpu.VMEM((rounds, tile, STEP), bf16),
@@ -298,16 +330,15 @@
             pltpu.VMEM((quarter, members, half, tile), bf16),
             pltpu.VMEM((quarter, tile, tile), bf16),
             pltpu.VMEM((2, tile, tile), bf16),
-            pltpu.VMEM((members, members * members), jnp.float32),
-            pltpu.SMEM((members, members * members), jnp.float32),
+            pltpu.VMEM((quarter * members * BAND, members * BAND), bf16),
             dma((groups,)), dma((groups,)),
             dma((4,)), dma((members,)),
             dma((rounds, 4)), dma((rounds, members)),
             dma((rounds, quarter)), dma((rounds, 2)),
-            dma,
+            dma((5,)), dma((rounds,)),
         ],
         compiler_params=pltpu.CompilerParams(
-            collective_id=0, has_side_effects=True, vmem_limit_bytes=40 * 1024 * 1024
+            collective_id=0, has_side_effects=True, vmem_limit_bytes=VMEM_BYTES
         ),
     )(amplitudes, integrals, jnp.transpose(task_list, (2, 0, 1)), task_counts, owner_map)
 

time: 46.1 us -> 43.5 us (0.944)
  local copies, waits for them, and re-layouts: 4 us -> 1.71 us
    unnamed x11 -> x1, local copies, waits for them, and re-layouts: 4 us -> 1.71 us
where the time goes in v2:
time: 43.5 us; the launch traced here: 43.4 us
  Pallas kernels  41.7 us (96%)
  local copies, waits for them, and re-layouts  1.71 us (4%)
    pallas_call x1, Pallas kernels, local_workers(): pl.pallas_call(functools.partial(cycle_kernel, groups, members), out_shap...  41.7 us
    unnamed x1, local copies, waits for them, and re-layouts  1.71 us

profile of v2, /device:TPU:0, one launch (start us, length us, event | category | flops | bytes accessed | tf_op | source)
XLA Modules:
  0.0 43.4 jit_solution(2260831766573404758)
XLA Ops:
  0.0 41.7 %shard_map.55 = bf16[1,1,384,384]{3,2,1,0:T(8,128)(2,1)} custom-call(bf16[1,1,384,384]{3,2,1,0:T(8,128)(2,1)} %amp_hbm.1, bf16[1,1,384,384]{3,2,1,0:T(8,128)(2,1)} %integ.1, s32[3,1,512]{2,1,0:T(1,128)} %bitcast.1, s32[1,8]{1,0:T(1,128)} %counts_hbm.1, s32[8]{0:T(128)} %owner_hbm.1), custom_call_target="tpu_custom_call" | custom-call | tf_op jit(solution)/shard_map/pallas_call | solution.py:315
  41.7 1.7 %copy.7 = bf16[1,1,384,384]{3,2,1,0:T(8,128)(2,1)} copy(bf16[1,1,384,384]{3,2,1,0:T(8,128)(2,1)} %shard_map.55) | data formatting | bytes 589824

commit v3 on v2

--- a/solution.py
+++ b/solution.py
@@ -120,7 +120,6 @@
     half, block, rounds = tile // 2, tile // groups, tile // STEP
     quarter = members // 2
     first_worker = members // 2 - 2
-    workers = range(first_worker, first_worker + 4)
     plane, side = lax.div(mem, 2), lax.rem(mem, 2)
     area = lax.div(mem, quarter)
     works = (mem >= first_worker) & (mem < first_worker + 4)
@@ -157,17 +156,46 @@
             swap.at[grp], swap_ss.at[peer], swap_rs.at[grp], grp=peer,
         )
 
-    def int_copy(index, worker):
-        return remote(
-            integ.at[0, 0, pl.ds((worker % 2) * half, half)],
-            halves.at[mem], int_ss.at[index], int_rs.at[mem], mem=worker,
-        )
-
-    def mix_copy(turn, index, worker):
-        return remote(
-            mixed_t.at[turn, pl.ds((worker % 2) * half, half)],
-            got_t.at[turn, mem], mix_ss.at[turn, index], mix_rs.at[turn, mem], mem=worker,
-        )
+    partner = mem + 1 - 2 * side
+    other_rows = pl.ds(pl.multiple_of((1 - side) * half, half), half)
+    lines = [(first_worker // 2 + index) * 2 + side for index in range(2)]
+
+    def int_copy(index):
+        if index == 0:
+            source, slot, target = integ.at[0, 0, other_rows], mem, partner
+        elif index < 3:
+            source, slot, target = integ.at[0, 0, own_rows], mem, lines[index - 1]
+        else:
+            source, slot, target = halves.at[partner], partner, lines[index - 3]
+        return remote(source, halves.at[slot], int_ss.at[index], int_rs.at[slot], mem=target)
+
+    def mix_copy(turn, index):
+        if index == 0:
+            source, slot, target = mixed_t.at[turn, other_rows], mem, partner
+        elif index < 3:
+            source, slot, target = mixed_t.at[turn, own_rows], mem, lines[index - 1]
+        else:
+            source, slot, target = got_t.at[turn, partner], partner, lines[index - 3]
+        return remote(
+            source, got_t.at[turn, slot], mix_ss.at[turn, index], mix_rs.at[turn, slot], mem=target
+        )
+
+    def int_arrival(source):
+        return remote(
+            halves.at[source], halves.at[source], int_ss.at[0], int_rs.at[source], mem=partner
+        )
+
+    def mix_arrival(turn, source):
+        return remote(
+            got_t.at[turn, source], got_t.at[turn, source],
+            mix_ss.at[turn, 0], mix_rs.at[turn, source], mem=partner,
+        )
+
+    def along_lines(first, do):
+        for index in range(2):
+            @pl.when(mem != lines[index])
+            def _():
+                do(first + index)
 
     def part_copy(turn, index, target):
         rows = pl.ds(turn * STEP, STEP)
@@ -182,10 +210,8 @@
 
     for turn in range(1, groups):
         swap_copy(lax.rem(grp + turn, groups)).start()
-    for index, worker in enumerate(workers):
-        @pl.when(mem != worker)
-        def _():
-            int_copy(index, worker).start()
+    int_copy(0).start()
+    along_lines(1, lambda index: int_copy(index).start())
 
     amp_in.wait()
     own_block = pl.ds(pl.multiple_of(grp * block, block), block)
@@ -199,6 +225,8 @@
         half_in.wait()
         spread[...] = spread_counts(members, quarter, area, tasks, counts, owner)
 
+    int_arrival(partner).wait_recv()
+    along_lines(3, lambda index: int_copy(index).start())
     for turn in range(1, groups):
         peer = lax.rem(grp + turn, groups)
         remote(
@@ -211,24 +239,23 @@
             2.0 * amp[0, 0, rows].astype(jnp.float32) - swapped.astype(jnp.float32)
         )
         mixed_t[turn] = mixed.T.astype(jnp.bfloat16)
-        for index, worker in enumerate(workers):
-            @pl.when(mem != worker)
-            def _():
-                mix_copy(turn, index, worker).start()
+        mix_copy(turn, 0).start()
+        along_lines(1, lambda index: mix_copy(turn, index).start())
 
         @pl.when(works)
         def _():
             got_t[turn, mem] = mixed_t[turn, own_rows]
 
+    for turn in range(rounds):
+        mix_arrival(turn, partner).wait_recv()
+        along_lines(3, lambda index: mix_copy(turn, index).start())
+
     @pl.when(works)
     def _():
         for source in range(members):
-            @pl.when(mem != source)
+            @pl.when(plane != source // 2)
             def _():
-                remote(
-                    halves.at[source], halves.at[source],
-                    int_ss.at[0], int_rs.at[source], mem=source,
-                ).wait_recv()
+                int_arrival(source).wait_recv()
 
         def weigh(index, carry):
             rows = pl.ds(pl.multiple_of(index * BAND, BAND), BAND)
@@ -244,12 +271,9 @@
         for turn in range(rounds):
             rows = pl.ds(turn * STEP, STEP)
             for source in range(members):
-                @pl.when(mem != source)
+                @pl.when(plane != source // 2)
                 def _():
-                    remote(
-                        got_t.at[turn, source], got_t.at[turn, source],
-                        mix_ss.at[turn, 0], mix_rs.at[turn, source], mem=source,
-                    ).wait_recv()
+                    mix_arrival(turn, source).wait_recv()
             left = got_t[turn].reshape(members * half, STEP).T
             for q in range(quarter):
                 target = area * quarter + q
@@ -284,12 +308,13 @@
 
     for turn in range(1, groups):
         swap_copy(lax.rem(grp + turn, groups)).wait_send()
-    for index, worker in enumerate(workers):
-        @pl.when(mem != worker)
-        def _():
-            int_copy(index, worker).wait_send()
-            for turn in range(rounds):
-                mix_copy(turn, index, worker).wait_send()
+    int_copy(0).wait_send()
+    along_lines(1, lambda index: int_copy(index).wait_send())
+    along_lines(3, lambda index: int_copy(index).wait_send())
+    for turn in range(rounds):
+        mix_copy(turn, 0).wait_send()
+        along_lines(1, lambda index: mix_copy(turn, index).wait_send())
+        along_lines(3, lambda index: mix_copy(turn, index).wait_send())
 
     @pl.when(works)
     def _():
@@ -332,8 +357,8 @@
             pltpu.VMEM((2, tile, tile), bf16),
             pltpu.VMEM((quarter * members * BAND, members * BAND), bf16),
             dma((groups,)), dma((groups,)),
-            dma((4,)), dma((members,)),
-            dma((rounds, 4)), dma((rounds, members)),
+            dma((5,)), dma((members,)),
+            dma((rounds, 5)), dma((rounds, members)),
             dma((rounds, quarter)), dma((rounds, 2)),
             dma((5,)), dma((rounds,)),
         ],

time: 43.5 us -> 45.1 us (1.037)
  Pallas kernels: 41.7 us -> 43.3 us
    pallas_call x1, Pallas kernels: 41.7 us -> 43.3 us  [local_workers(): pl.pallas_call(functools.partial(cycle_kernel, groups, members), out_shap...]
where the time goes in v3:
time: 45.1 us; the launch traced here: 45 us
  Pallas kernels  43.3 us (96%)
  local copies, waits for them, and re-layouts  1.71 us (4%)
    pallas_call x1, Pallas kernels, local_workers(): pl.pallas_call(functools.partial(cycle_kernel, groups, members), out_shap...  43.3 us
    unnamed x1, local copies, waits for them, and re-layouts  1.71 us

profile of v3, /device:TPU:0, one launch (start us, length us, event | category | flops | bytes accessed | tf_op | source)
XLA Modules:
  0.0 45.0 jit_solution(1924601788360404604)
XLA Ops:
  0.0 43.3 %shard_map.55 = bf16[1,1,384,384]{3,2,1,0:T(8,128)(2,1)} custom-call(bf16[1,1,384,384]{3,2,1,0:T(8,128)(2,1)} %amp_hbm.1, bf16[1,1,384,384]{3,2,1,0:T(8,128)(2,1)} %integ.1, s32[3,1,512]{2,1,0:T(1,128)} %bitcast.1, s32[1,8]{1,0:T(1,128)} %counts_hbm.1, s32[8]{0:T(128)} %owner_hbm.1), custom_call_target="tpu_custom_call" | custom-call | tf_op jit(solution)/shard_map/pallas_call | solution.py:340
  43.3 1.7 %copy.7 = bf16[1,1,384,384]{3,2,1,0:T(8,128)(2,1)} copy(bf16[1,1,384,384]{3,2,1,0:T(8,128)(2,1)} %shard_map.55) | data formatting | bytes 589824

commit v4 on v2

--- a/solution.py
+++ b/solution.py
@@ -211,14 +211,26 @@
             2.0 * amp[0, 0, rows].astype(jnp.float32) - swapped.astype(jnp.float32)
         )
         mixed_t[turn] = mixed.T.astype(jnp.bfloat16)
-        for index, worker in enumerate(workers):
-            @pl.when(mem != worker)
-            def _():
-                mix_copy(turn, index, worker).start()
-
         @pl.when(works)
         def _():
             got_t[turn, mem] = mixed_t[turn, own_rows]
+
+    def send_mixed(turn):
+        for index, worker in enumerate(workers):
+            @pl.when(mem != worker)
+            def _():
+                (mix_copy(turn - 1, index, worker) if turn else int_copy(index, worker)).wait_send()
+        for index, worker in enumerate(workers):
+            @pl.when(mem != worker)
+            def _():
+                mix_copy(turn, index, worker).start()
+
+    send_mixed(0)
+
+    @pl.when(jnp.logical_not(works))
+    def _():
+        for turn in range(1, rounds):
+            send_mixed(turn)
 
     @pl.when(works)
     def _():
@@ -243,6 +255,8 @@
 
         for turn in range(rounds):
             rows = pl.ds(turn * STEP, STEP)
+            if turn + 1 < rounds:
+                send_mixed(turn + 1)
             for source in range(members):
                 @pl.when(mem != source)
                 def _():
@@ -287,9 +301,7 @@
     for index, worker in enumerate(workers):
         @pl.when(mem != worker)
         def _():
-            int_copy(index, worker).wait_send()
-            for turn in range(rounds):
-                mix_copy(turn, index, worker).wait_send()
+            mix_copy(rounds - 1, index, worker).wait_send()
 
     @pl.when(works)
     def _():

time: 43.5 us -> 45.4 us (1.044)
  Pallas kernels: 41.7 us -> 43.5 us
    pallas_call x1, Pallas kernels: 41.7 us -> 43.5 us  [local_workers(): pl.pallas_call(functools.partial(cycle_kernel, groups, members), out_shap...]
where the time goes in v4:
time: 45.4 us; the launch traced here: 45.3 us
  Pallas kernels  43.5 us (96%)
  local copies, waits for them, and re-layouts  1.71 us (4%)
    pallas_call x1, Pallas kernels, local_workers(): pl.pallas_call(functools.partial(cycle_kernel, groups, members), out_shap...  43.5 us
    unnamed x1, local copies, waits for them, and re-layouts  1.71 us

profile of v4, /device:TPU:0, one launch (start us, length us, event | category | flops | bytes accessed | tf_op | source)
XLA Modules:
  0.0 45.3 jit_solution(8087032398743907138)
XLA Ops:
  0.0 43.5 %shard_map.55 = bf16[1,1,384,384]{3,2,1,0:T(8,128)(2,1)} custom-call(bf16[1,1,384,384]{3,2,1,0:T(8,128)(2,1)} %amp_hbm.1, bf16[1,1,384,384]{3,2,1,0:T(8,128)(2,1)} %integ.1, s32[3,1,512]{2,1,0:T(1,128)} %bitcast.1, s32[1,8]{1,0:T(1,128)} %counts_hbm.1, s32[8]{0:T(128)} %owner_hbm.1), custom_call_target="tpu_custom_call" | custom-call | tf_op jit(solution)/shard_map/pallas_call | solution.py:327
  43.5 1.7 %copy.7 = bf16[1,1,384,384]{3,2,1,0:T(8,128)(2,1)} copy(bf16[1,1,384,384]{3,2,1,0:T(8,128)(2,1)} %shard_map.55) | data formatting | bytes 589824

commit v5 on v2

--- a/solution.py
+++ b/solution.py
@@ -78,7 +78,7 @@
     )
 
 
-def spread_counts(members, quarter, area, tasks, counts, owner):
+def spread_counts(members, tasks, counts, owner):
     total = tasks.shape[-1]
     slots = total // members
     ids = [tasks[field] for field in range(3)]
@@ -92,9 +92,9 @@
         offset = place - executor * slots
         inside = (offset >= 0) & (offset < jnp.minimum(counts[0, executor], slots))
         live = jnp.where(inside, 1, live)
-    key = (rows[0] - area * quarter) * members + rows[1]
+    key = rows[0] * members + rows[1]
     key = jnp.where(live == 1, key, -1)
-    tall, wide = quarter * members * BAND, members * BAND
+    tall, wide = members * members * BAND, members * BAND
     hot_left = lax.broadcasted_iota(jnp.int32, (tall, total), 0) // BAND == key
     hot_right = lax.broadcasted_iota(jnp.int32, (wide, total), 0) // BAND == rows[2]
     spread = lax.dot_general(
@@ -111,19 +111,17 @@
 def cycle_kernel(
     groups, members,
     amp_hbm, integ, tasks_hbm, counts_hbm, owner_hbm, out,
-    amp, tasks, counts, owner, result,
-    swap, halves, mixed_t, got_t, weighed, parts, landed, spread,
-    swap_ss, swap_rs, int_ss, int_rs, mix_ss, mix_rs, part_ss, part_rs, local_sem, out_sem,
+    amp, tasks, counts, owner,
+    swap, halves, mixed_t, got_t, weighed, given, taken, kept, final, spread,
+    swap_ss, swap_rs, int_ss, int_rs, mix_ss, mix_rs, part_ss, part_rs, out_ss, out_rs, local_sem,
 ):
     grp, mem = lax.axis_index("grp"), lax.axis_index("mem")
     tile = amp.shape[-1]
-    half, block, rounds = tile // 2, tile // groups, tile // STEP
-    quarter = members // 2
-    first_worker = members // 2 - 2
-    workers = range(first_worker, first_worker + 4)
+    half, block, rounds, planes = tile // 2, tile // groups, tile // STEP, members // 2
     plane, side = lax.div(mem, 2), lax.rem(mem, 2)
-    area = lax.div(mem, quarter)
-    works = (mem >= first_worker) & (mem < first_worker + 4)
+    partner = mem + 1 - 2 * side
+    work_plane = planes // 2 - 1 + lax.rem(grp, 2)
+    works = plane == work_plane
     own_rows = pl.ds(pl.multiple_of(side * half, half), half)
 
     amp_in = pltpu.make_async_copy(amp_hbm, amp, local_sem.at[0])
@@ -145,11 +143,22 @@
         pl.semaphore_signal(
             barrier, inc=1, device_id={"grp": lax.rem(grp + turn, groups)}, device_id_type=MESH
         )
-    for turn in range(1, members):
-        pl.semaphore_signal(
-            barrier, inc=1, device_id={"mem": lax.rem(mem + turn, members)}, device_id_type=MESH
-        )
-    pl.semaphore_wait(barrier, groups + members - 2)
+
+    @pl.when(works)
+    def _():
+        for turn in range(1, members):
+            pl.semaphore_signal(
+                barrier, inc=1, device_id={"mem": lax.rem(mem + turn, members)}, device_id_type=MESH
+            )
+        pl.semaphore_wait(barrier, groups + members - 2)
+
+    @pl.when(jnp.logical_not(works))
+    def _():
+        for worker_side in range(2):
+            pl.semaphore_signal(
+                barrier, inc=1, device_id={"mem": work_plane * 2 + worker_side}, device_id_type=MESH
+            )
+        pl.semaphore_wait(barrier, groups + 1)
 
     def swap_copy(peer):
         return remote(
@@ -157,47 +166,50 @@
             swap.at[grp], swap_ss.at[peer], swap_rs.at[grp], grp=peer,
         )
 
-    def int_copy(index, worker):
-        return remote(
-            integ.at[0, 0, pl.ds((worker % 2) * half, half)],
-            halves.at[mem], int_ss.at[index], int_rs.at[mem], mem=worker,
-        )
-
-    def mix_copy(turn, index, worker):
-        return remote(
-            mixed_t.at[turn, pl.ds((worker % 2) * half, half)],
-            got_t.at[turn, mem], mix_ss.at[turn, index], mix_rs.at[turn, mem], mem=worker,
-        )
-
-    def part_copy(turn, index, target):
-        rows = pl.ds(turn * STEP, STEP)
-        return remote(
-            parts.at[index, rows], landed.at[side, rows],
-            part_ss.at[turn, index], part_rs.at[turn, side], mem=target,
-        )
-
-    def result_copy(turn):
-        rows = pl.ds(turn * STEP, STEP)
-        return pltpu.make_async_copy(result.at[rows], out.at[0, 0, rows], out_sem.at[turn])
+    def int_copy(worker_side):
+        return remote(
+            integ.at[0, 0, pl.ds(worker_side * half, half)],
+            halves.at[mem], int_ss.at[worker_side], int_rs.at[mem],
+            mem=work_plane * 2 + worker_side,
+        )
+
+    def mix_copy(turn, worker_side):
+        return remote(
+            mixed_t.at[turn, pl.ds(worker_side * half, half)],
+            got_t.at[turn, mem], mix_ss.at[turn, worker_side], mix_rs.at[turn, mem],
+            mem=work_plane * 2 + worker_side,
+        )
+
+    def part_copy(turn, row):
+        return remote(
+            given.at[turn, row], taken.at[turn, row],
+            part_ss.at[turn, row], part_rs.at[turn, row], mem=partner,
+        )
+
+    def out_copy(turn, row):
+        return remote(
+            final.at[turn, row], out.at[0, 0, pl.ds(turn * STEP, STEP)],
+            out_ss.at[turn, row], out_rs.at[turn], mem=row * 2 + side,
+        )
+
+    def own_copy(turn):
+        return pltpu.make_async_copy(
+            final.at[turn, plane], out.at[0, 0, pl.ds(turn * STEP, STEP)], out_rs.at[turn]
+        )
+
+    def to_workers(do):
+        for worker_side in range(2):
+            @pl.when(mem != work_plane * 2 + worker_side)
+            def _():
+                do(worker_side)
 
     for turn in range(1, groups):
         swap_copy(lax.rem(grp + turn, groups)).start()
-    for index, worker in enumerate(workers):
-        @pl.when(mem != worker)
-        def _():
-            int_copy(index, worker).start()
+    to_workers(lambda worker_side: int_copy(worker_side).start())
 
     amp_in.wait()
     own_block = pl.ds(pl.multiple_of(grp * block, block), block)
     swap[grp] = amp[0, 0, own_block]
-
-    @pl.when(works)
-    def _():
-        tasks_in.wait()
-        counts_in.wait()
-        owner_in.wait()
-        half_in.wait()
-        spread[...] = spread_counts(members, quarter, area, tasks, counts, owner)
 
     for turn in range(1, groups):
         peer = lax.rem(grp + turn, groups)
@@ -211,10 +223,7 @@
             2.0 * amp[0, 0, rows].astype(jnp.float32) - swapped.astype(jnp.float32)
         )
         mixed_t[turn] = mixed.T.astype(jnp.bfloat16)
-        for index, worker in enumerate(workers):
-            @pl.when(mem != worker)
-            def _():
-                mix_copy(turn, index, worker).start()
+        to_workers(lambda worker_side: mix_copy(turn, worker_side).start())
 
         @pl.when(works)
         def _():
@@ -222,12 +231,17 @@
 
     @pl.when(works)
     def _():
+        tasks_in.wait()
+        counts_in.wait()
+        owner_in.wait()
+        half_in.wait()
+        spread[...] = spread_counts(members, tasks, counts, owner)
         for source in range(members):
             @pl.when(mem != source)
             def _():
                 remote(
                     halves.at[source], halves.at[source],
-                    int_ss.at[0], int_rs.at[source], mem=source,
+                    int_ss.at[0], int_rs.at[source], mem=partner,
                 ).wait_recv()
 
         def weigh(index, carry):
@@ -236,79 +250,75 @@
                 spread[...], halves[:, rows].reshape(members * BAND, tile),
                 preferred_element_type=jnp.float32,
             )
-            weighed[:, :, rows] = sums.astype(jnp.bfloat16).reshape(quarter, members, BAND, tile)
+            weighed[:, :, rows] = sums.astype(jnp.bfloat16).reshape(members, members, BAND, tile)
             return carry
 
         lax.fori_loop(0, half // BAND, weigh, 0)
 
+        def finish(turn):
+            for row in range(planes):
+                part_copy(turn, row).wait_recv()
+                final[turn, row] = (
+                    kept[turn, row] + taken[turn, row].astype(jnp.float32)
+                ).astype(jnp.bfloat16)
+
+                @pl.when(plane != row)
+                def _():
+                    out_copy(turn, row).start()
+
+                @pl.when(plane == row)
+                def _():
+                    own_copy(turn).start()
+
         for turn in range(rounds):
-            rows = pl.ds(turn * STEP, STEP)
             for source in range(members):
                 @pl.when(mem != source)
                 def _():
                     remote(
                         got_t.at[turn, source], got_t.at[turn, source],
-                        mix_ss.at[turn, 0], mix_rs.at[turn, source], mem=source,
+                        mix_ss.at[turn, 0], mix_rs.at[turn, source], mem=partner,
                     ).wait_recv()
             left = got_t[turn].reshape(members * half, STEP).T
-            for q in range(quarter):
-                target = area * quarter + q
-                parts[q, rows] = jnp.dot(
-                    left, weighed[q].reshape(members * half, tile),
+
+            def multiply(target):
+                return jnp.dot(
+                    left, weighed[target].reshape(members * half, tile),
                     preferred_element_type=jnp.float32,
-                ).astype(jnp.bfloat16)
-
-                @pl.when(mem != target)
+                )
+
+            for row in range(planes):
+                given[turn, row] = multiply(row * 2 + 1 - side).astype(jnp.bfloat16)
+                part_copy(turn, row).start()
+            for row in range(planes):
+                kept[turn, row] = multiply(row * 2 + side)
+            if turn:
+                finish(turn - 1)
+        finish(rounds - 1)
+        for turn in range(rounds):
+            own_copy(turn).wait()
+            for row in range(planes):
+                part_copy(turn, row).wait_send()
+
+                @pl.when(plane != row)
                 def _():
-                    part_copy(turn, q, target).start()
-
-                @pl.when(mem == target)
-                def _():
-                    landed[side, rows] = parts[q, rows]
-
-    for turn in range(rounds):
-        rows = pl.ds(turn * STEP, STEP)
-        for sender_side in range(2):
-            sender = lax.min(lax.max(plane, quarter // 2 - 1), quarter // 2) * 2 + sender_side
-
-            @pl.when(mem != sender)
-            def _():
-                remote(
-                    landed.at[sender_side, rows], landed.at[sender_side, rows],
-                    part_ss.at[turn, 0], part_rs.at[turn, sender_side], mem=sender,
-                ).wait_recv()
-        result[rows] = (
-            landed[0, rows].astype(jnp.float32) + landed[1, rows].astype(jnp.float32)
-        ).astype(jnp.bfloat16)
-        result_copy(turn).start()
+                    out_copy(turn, row).wait_send()
+
+    @pl.when(jnp.logical_not(works))
+    def _():
+        for turn in range(rounds):
+            out_copy(turn, 0).wait_recv()
 
     for turn in range(1, groups):
         swap_copy(lax.rem(grp + turn, groups)).wait_send()
-    for index, worker in enumerate(workers):
-        @pl.when(mem != worker)
-        def _():
-            int_copy(index, worker).wait_send()
-            for turn in range(rounds):
-                mix_copy(turn, index, worker).wait_send()
-
-    @pl.when(works)
-    def _():
-        for q in range(quarter):
-            target = area * quarter + q
-
-            @pl.when(mem != target)
-            def _():
-                for turn in range(rounds):
-                    part_copy(turn, q, target).wait_send()
-
+    to_workers(lambda worker_side: int_copy(worker_side).wait_send())
     for turn in range(rounds):
-        result_copy(turn).wait()
+        to_workers(lambda worker_side: mix_copy(turn, worker_side).wait_send())
 
 
 def local_workers(amplitudes, integrals, task_list, task_counts, owner_map):
     groups, members = lax.axis_size("grp"), lax.axis_size("mem")
     tile = amplitudes.shape[-1]
-    half, rounds, quarter = tile // 2, tile // STEP, members // 2
+    half, rounds, planes = tile // 2, tile // STEP, members // 2
     hbm = pl.BlockSpec(memory_space=pltpu.HBM)
     dma = pltpu.SemaphoreType.DMA
     bf16 = jnp.bfloat16
@@ -322,20 +332,22 @@
             pltpu.VMEM((3, 1, task_list.shape[1]), jnp.int32),
             pltpu.SMEM(task_counts.shape, jnp.int32),
             pltpu.SMEM(owner_map.shape, jnp.int32),
-            pltpu.VMEM((tile, tile), bf16),
             pltpu.VMEM((groups, tile // groups, tile), bf16),
             pltpu.VMEM((members, half, tile), bf16),
             pltpu.VMEM((rounds, tile, STEP), bf16),
             pltpu.VMEM((rounds, members, half, STEP), bf16),
-            pltpu.VMEM((quarter, members, half, tile), bf16),
-            pltpu.VMEM((quarter, tile, tile), bf16),
-            pltpu.VMEM((2, tile, tile), bf16),
-            pltpu.VMEM((quarter * members * BAND, members * BAND), bf16),
+            pltpu.VMEM((members, members, half, tile), bf16),
+            pltpu.VMEM((rounds, planes, STEP, tile), bf16),
+            pltpu.VMEM((rounds, planes, STEP, tile), bf16),
+            pltpu.VMEM((rounds, planes, STEP, tile), jnp.float32),
+            pltpu.VMEM((rounds, planes, STEP, tile), bf16),
+            pltpu.VMEM((members * members * BAND, members * BAND), bf16),
             dma((groups,)), dma((groups,)),
-            dma((4,)), dma((members,)),
-            dma((rounds, 4)), dma((rounds, members)),
-            dma((rounds, quarter)), dma((rounds, 2)),
-            dma((5,)), dma((rounds,)),
+            dma((2,)), dma((members,)),
+            dma((rounds, 2)), dma((rounds, members)),
+            dma((rounds, planes)), dma((rounds, planes)),
+            dma((rounds, planes)), dma((rounds,)),
+            dma((5,)),
         ],
         compiler_params=pltpu.CompilerParams(
             collective_id=0, has_side_effects=True, vmem_limit_bytes=VMEM_BYTES

time: 43.5 us -> 38.5 us (0.89); the launches traced: 43.4 us -> 37.9 us
  Pallas kernels: 41.7 us -> 36.2 us
    pallas_call x1, Pallas kernels: 41.7 us -> 36.2 us  [local_workers(): pl.pallas_call(functools.partial(cycle_kernel, groups, members), out_shap...]
where the time goes in v5:
time: 38.5 us; the launch traced here: 37.9 us
  Pallas kernels  36.2 us (94%)
  local copies, waits for them, and re-layouts  1.71 us (4%)
    pallas_call x1, Pallas kernels, local_workers(): pl.pallas_call(functools.partial(cycle_kernel, groups, members), out_shap...  36.2 us
    unnamed x1, local copies, waits for them, and re-layouts  1.71 us

profile of v5, /device:TPU:0, one launch (start us, length us, event | category | flops | bytes accessed | tf_op | source)
XLA Modules:
  0.0 37.9 jit_solution(15844151258087970308)
XLA Ops:
  0.0 36.2 %shard_map.55 = bf16[1,1,384,384]{3,2,1,0:T(8,128)(2,1)} custom-call(bf16[1,1,384,384]{3,2,1,0:T(8,128)(2,1)} %amp_hbm.1, bf16[1,1,384,384]{3,2,1,0:T(8,128)(2,1)} %integ.1, s32[3,1,512]{2,1,0:T(1,128)} %bitcast.1, s32[1,8]{1,0:T(1,128)} %counts_hbm.1, s32[8]{0:T(128)} %owner_hbm.1), custom_call_target="tpu_custom_call" | custom-call | tf_op jit(solution)/shard_map/pallas_call | solution.py:325
  36.2 1.7 %copy.7 = bf16[1,1,384,384]{3,2,1,0:T(8,128)(2,1)} copy(bf16[1,1,384,384]{3,2,1,0:T(8,128)(2,1)} %shard_map.55) | data formatting | bytes 589824

commit v6 on v5

--- a/solution.py
+++ b/solution.py
@@ -66,7 +66,8 @@
 
 
 MESH = pl.DeviceIdType.MESH
-STEP = 128
+STEP = 64
+PIECE = 128
 BAND = 32
 VMEM_BYTES = 65280 * 1024
 
@@ -92,11 +93,11 @@
         offset = place - executor * slots
         inside = (offset >= 0) & (offset < jnp.minimum(counts[0, executor], slots))
         live = jnp.where(inside, 1, live)
-    key = rows[0] * members + rows[1]
+    key = rows[2] * members + rows[0]
     key = jnp.where(live == 1, key, -1)
     tall, wide = members * members * BAND, members * BAND
     hot_left = lax.broadcasted_iota(jnp.int32, (tall, total), 0) // BAND == key
-    hot_right = lax.broadcasted_iota(jnp.int32, (wide, total), 0) // BAND == rows[2]
+    hot_right = lax.broadcasted_iota(jnp.int32, (wide, total), 0) // BAND == rows[1]
     spread = lax.dot_general(
         jnp.where(hot_left, 1.0, 0.0).astype(jnp.bfloat16),
         jnp.where(hot_right, 1.0, 0.0).astype(jnp.bfloat16),
@@ -112,23 +113,23 @@
     groups, members,
     amp_hbm, integ, tasks_hbm, counts_hbm, owner_hbm, out,
     amp, tasks, counts, owner,
-    swap, halves, mixed_t, got_t, weighed, given, taken, kept, final, spread,
-    swap_ss, swap_rs, int_ss, int_rs, mix_ss, mix_rs, part_ss, part_rs, out_ss, out_rs, local_sem,
+    swap, mixed, got_int, got_mix, weighed, final, spread,
+    swap_ss, swap_rs, int_ss, int_rs, pass_ss, mix_ss, mix_rs, out_ss, out_rs, own_sem, local_sem,
 ):
     grp, mem = lax.axis_index("grp"), lax.axis_index("mem")
     tile = amp.shape[-1]
-    half, block, rounds, planes = tile // 2, tile // groups, tile // STEP, members // 2
+    half, block, planes = tile // 2, tile // groups, members // 2
+    rounds, pieces = half // STEP, tile // PIECE
     plane, side = lax.div(mem, 2), lax.rem(mem, 2)
     partner = mem + 1 - 2 * side
     work_plane = planes // 2 - 1 + lax.rem(grp, 2)
     works = plane == work_plane
-    own_rows = pl.ds(pl.multiple_of(side * half, half), half)
 
     amp_in = pltpu.make_async_copy(amp_hbm, amp, local_sem.at[0])
     tasks_in = pltpu.make_async_copy(tasks_hbm, tasks, local_sem.at[1])
     counts_in = pltpu.make_async_copy(counts_hbm, counts, local_sem.at[2])
     owner_in = pltpu.make_async_copy(owner_hbm, owner, local_sem.at[3])
-    half_in = pltpu.make_async_copy(integ.at[0, 0, own_rows], halves.at[mem], local_sem.at[4])
+    int_in = pltpu.make_async_copy(integ.at[0, 0], got_int.at[mem], local_sem.at[4])
     amp_in.start()
 
     @pl.when(works)
@@ -136,7 +137,7 @@
         tasks_in.start()
         counts_in.start()
         owner_in.start()
-        half_in.start()
+        int_in.start()
 
     barrier = pltpu.get_barrier_semaphore()
     for turn in range(1, groups):
@@ -166,35 +167,52 @@
             swap.at[grp], swap_ss.at[peer], swap_rs.at[grp], grp=peer,
         )
 
-    def int_copy(worker_side):
-        return remote(
-            integ.at[0, 0, pl.ds(worker_side * half, half)],
-            halves.at[mem], int_ss.at[worker_side], int_rs.at[mem],
+    def int_copy(piece):
+        rows = pl.ds(piece * PIECE, PIECE)
+        return remote(
+            integ.at[0, 0, rows], got_int.at[mem, rows], int_ss.at[piece], int_rs.at[piece, mem],
+            mem=jnp.where(works, partner, work_plane * 2 + side),
+        )
+
+    def pass_copy(piece, row):
+        source, rows = row * 2 + side, pl.ds(piece * PIECE, PIECE)
+        return remote(
+            got_int.at[source, rows], got_int.at[source, rows],
+            pass_ss.at[piece, row], int_rs.at[piece, source], mem=partner,
+        )
+
+    def int_arrival(piece, source):
+        rows = pl.ds(piece * PIECE, PIECE)
+        return remote(
+            got_int.at[source, rows], got_int.at[source, rows],
+            int_ss.at[piece], int_rs.at[piece, source], mem=partner,
+        )
+
+    def mix_copy(turn, worker_side):
+        return remote(
+            mixed.at[pl.ds(worker_side * half + turn * STEP, STEP)],
+            got_mix.at[turn, mem], mix_ss.at[turn, worker_side], mix_rs.at[turn, mem],
             mem=work_plane * 2 + worker_side,
         )
 
-    def mix_copy(turn, worker_side):
-        return remote(
-            mixed_t.at[turn, pl.ds(worker_side * half, half)],
-            got_t.at[turn, mem], mix_ss.at[turn, worker_side], mix_rs.at[turn, mem],
-            mem=work_plane * 2 + worker_side,
-        )
-
-    def part_copy(turn, row):
-        return remote(
-            given.at[turn, row], taken.at[turn, row],
-            part_ss.at[turn, row], part_rs.at[turn, row], mem=partner,
-        )
-
-    def out_copy(turn, row):
-        return remote(
-            final.at[turn, row], out.at[0, 0, pl.ds(turn * STEP, STEP)],
-            out_ss.at[turn, row], out_rs.at[turn], mem=row * 2 + side,
+    def out_rows(turn, worker_side):
+        return pl.ds(pl.multiple_of(worker_side * half + turn * STEP, STEP), STEP)
+
+    def out_copy(turn, target):
+        return remote(
+            final.at[turn, target], out.at[0, 0, out_rows(turn, side)],
+            out_ss.at[turn, target], out_rs.at[turn, side], mem=target,
+        )
+
+    def out_arrival(turn, worker_side):
+        return remote(
+            final.at[turn, 0], out.at[0, 0, out_rows(turn, worker_side)],
+            out_ss.at[turn, 0], out_rs.at[turn, worker_side], mem=partner,
         )
 
     def own_copy(turn):
         return pltpu.make_async_copy(
-            final.at[turn, plane], out.at[0, 0, pl.ds(turn * STEP, STEP)], out_rs.at[turn]
+            final.at[turn, mem], out.at[0, 0, out_rows(turn, side)], own_sem.at[turn]
         )
 
     def to_workers(do):
@@ -205,7 +223,8 @@
 
     for turn in range(1, groups):
         swap_copy(lax.rem(grp + turn, groups)).start()
-    to_workers(lambda worker_side: int_copy(worker_side).start())
+    for piece in range(pieces):
+        int_copy(piece).start()
 
     amp_in.wait()
     own_block = pl.ds(pl.multiple_of(grp * block, block), block)
@@ -217,100 +236,90 @@
             swap.at[peer], swap.at[peer], swap_ss.at[peer], swap_rs.at[peer], grp=peer
         ).wait_recv()
     for turn in range(rounds):
-        rows = pl.ds(turn * STEP, STEP)
-        swapped = swap[...].reshape(tile, tile)[turn * STEP : (turn + 1) * STEP]
-        mixed = (
-            2.0 * amp[0, 0, rows].astype(jnp.float32) - swapped.astype(jnp.float32)
-        )
-        mixed_t[turn] = mixed.T.astype(jnp.bfloat16)
+        for worker_side in range(2):
+            first = worker_side * half + turn * STEP
+            rows = pl.ds(first, STEP)
+            swapped = swap[...].reshape(tile, tile)[first : first + STEP]
+            mixed[rows] = (
+                2.0 * amp[0, 0, rows].astype(jnp.float32) - swapped.astype(jnp.float32)
+            ).astype(jnp.bfloat16)
         to_workers(lambda worker_side: mix_copy(turn, worker_side).start())
 
-        @pl.when(works)
-        def _():
-            got_t[turn, mem] = mixed_t[turn, own_rows]
-
     @pl.when(works)
     def _():
+        for piece in range(pieces):
+            for row in range(planes):
+                @pl.when(plane != row)
+                def _():
+                    int_arrival(piece, row * 2 + side).wait_recv()
+                    pass_copy(piece, row).start()
+
         tasks_in.wait()
         counts_in.wait()
         owner_in.wait()
-        half_in.wait()
         spread[...] = spread_counts(members, tasks, counts, owner)
-        for source in range(members):
-            @pl.when(mem != source)
-            def _():
-                remote(
-                    halves.at[source], halves.at[source],
-                    int_ss.at[0], int_rs.at[source], mem=partner,
-                ).wait_recv()
-
-        def weigh(index, carry):
-            rows = pl.ds(pl.multiple_of(index * BAND, BAND), BAND)
-            sums = jnp.dot(
-                spread[...], halves[:, rows].reshape(members * BAND, tile),
-                preferred_element_type=jnp.float32,
-            )
-            weighed[:, :, rows] = sums.astype(jnp.bfloat16).reshape(members, members, BAND, tile)
-            return carry
-
-        lax.fori_loop(0, half // BAND, weigh, 0)
-
-        def finish(turn):
-            for row in range(planes):
-                part_copy(turn, row).wait_recv()
-                final[turn, row] = (
-                    kept[turn, row] + taken[turn, row].astype(jnp.float32)
-                ).astype(jnp.bfloat16)
-
-                @pl.when(plane != row)
-                def _():
-                    out_copy(turn, row).start()
-
-                @pl.when(plane == row)
-                def _():
-                    own_copy(turn).start()
+        for turn in range(rounds):
+            got_mix[turn, mem] = mixed[out_rows(turn, side)]
 
         for turn in range(rounds):
             for source in range(members):
                 @pl.when(mem != source)
                 def _():
                     remote(
-                        got_t.at[turn, source], got_t.at[turn, source],
+                        got_mix.at[turn, source], got_mix.at[turn, source],
                         mix_ss.at[turn, 0], mix_rs.at[turn, source], mem=partner,
                     ).wait_recv()
-            left = got_t[turn].reshape(members * half, STEP).T
-
-            def multiply(target):
-                return jnp.dot(
-                    left, weighed[target].reshape(members * half, tile),
-                    preferred_element_type=jnp.float32,
-                )
-
-            for row in range(planes):
-                given[turn, row] = multiply(row * 2 + 1 - side).astype(jnp.bfloat16)
-                part_copy(turn, row).start()
-            for row in range(planes):
-                kept[turn, row] = multiply(row * 2 + side)
-            if turn:
-                finish(turn - 1)
-        finish(rounds - 1)
+            for band in range(STEP // BAND):
+                rows = pl.ds(band * BAND, BAND)
+                read = got_mix[turn, :, rows].reshape(members * BAND, tile)
+                for b in range(members):
+                    sums = jnp.dot(
+                        spread[pl.ds(b * members * BAND, members * BAND)], read,
+                        preferred_element_type=jnp.float32,
+                    )
+                    weighed[:, rows, pl.ds(b * tile, tile)] = sums.astype(jnp.bfloat16).reshape(
+                        members, BAND, tile
+                    )
+            if turn == 0:
+                int_in.wait()
+                for piece in range(pieces):
+                    for row in range(planes):
+                        int_arrival(piece, row * 2 + 1 - side).wait_recv()
+            product = jnp.dot(
+                weighed[...].reshape(members * STEP, members * tile),
+                got_int[...].reshape(members * tile, tile),
+                preferred_element_type=jnp.float32,
+            )
+            final[turn] = product.astype(jnp.bfloat16).reshape(members, STEP, tile)
+            for target in range(members):
+                @pl.when(mem != target)
+                def _():
+                    out_copy(turn, target).start()
+            own_copy(turn).start()
+
         for turn in range(rounds):
             own_copy(turn).wait()
+            out_arrival(turn, 1 - side).wait_recv()
+            for target in range(members):
+                @pl.when(mem != target)
+                def _():
+                    out_copy(turn, target).wait_send()
+        for piece in range(pieces):
             for row in range(planes):
-                part_copy(turn, row).wait_send()
-
                 @pl.when(plane != row)
                 def _():
-                    out_copy(turn, row).wait_send()
+                    pass_copy(piece, row).wait_send()
 
     @pl.when(jnp.logical_not(works))
     def _():
         for turn in range(rounds):
-            out_copy(turn, 0).wait_recv()
+            for worker_side in range(2):
+                out_arrival(turn, worker_side).wait_recv()
 
     for turn in range(1, groups):
         swap_copy(lax.rem(grp + turn, groups)).wait_send()
-    to_workers(lambda worker_side: int_copy(worker_side).wait_send())
+    for piece in range(pieces):
+        int_copy(piece).wait_send()
     for turn in range(rounds):
         to_workers(lambda worker_side: mix_copy(turn, worker_side).wait_send())
 
@@ -318,7 +327,7 @@
 def local_workers(amplitudes, integrals, task_list, task_counts, owner_map):
     groups, members = lax.axis_size("grp"), lax.axis_size("mem")
     tile = amplitudes.shape[-1]
-    half, rounds, planes = tile // 2, tile // STEP, members // 2
+    rounds, pieces, planes = tile // 2 // STEP, tile // PIECE, members // 2
     hbm = pl.BlockSpec(memory_space=pltpu.HBM)
     dma = pltpu.SemaphoreType.DMA
     bf16 = jnp.bfloat16
@@ -333,20 +342,16 @@
             pltpu.SMEM(task_counts.shape, jnp.int32),
             pltpu.SMEM(owner_map.shape, jnp.int32),
             pltpu.VMEM((groups, tile // groups, tile), bf16),
-            pltpu.VMEM((members, half, tile), bf16),
-            pltpu.VMEM((rounds, tile, STEP), bf16),
-            pltpu.VMEM((rounds, members, half, STEP), bf16),
-            pltpu.VMEM((members, members, half, tile), bf16),
-            pltpu.VMEM((rounds, planes, STEP, tile), bf16),
-            pltpu.VMEM((rounds, planes, STEP, tile), bf16),
-            pltpu.VMEM((rounds, planes, STEP, tile), jnp.float32),
-            pltpu.VMEM((rounds, planes, STEP, tile), bf16),
+            pltpu.VMEM((tile, tile), bf16),
+            pltpu.VMEM((members, tile, tile), bf16),
+            pltpu.VMEM((rounds, members, STEP, tile), bf16),
+            pltpu.VMEM((members, STEP, members * tile), bf16),
+            pltpu.VMEM((rounds, members, STEP, tile), bf16),
             pltpu.VMEM((members * members * BAND, members * BAND), bf16),
             dma((groups,)), dma((groups,)),
-            dma((2,)), dma((members,)),
+            dma((pieces,)), dma((pieces, members)), dma((pieces, planes)),
             dma((rounds, 2)), dma((rounds, members)),
-            dma((rounds, planes)), dma((rounds, planes)),
-            dma((rounds, planes)), dma((rounds,)),
+            dma((rounds, members)), dma((rounds, 2)), dma((rounds,)),
             dma((5,)),
         ],
         compiler_params=pltpu.CompilerParams(

time: 38.5 us -> 42.7 us (1.11); the launches traced: 37.9 us -> 42.6 us
  Pallas kernels: 36.2 us -> 40.9 us
    pallas_call x1, Pallas kernels: 36.2 us -> 40.9 us  [local_workers(): pl.pallas_call(functools.partial(cycle_kernel, groups, members), out_shap...]
where the time goes in v6:
time: 42.7 us; the launch traced here: 42.6 us
  Pallas kernels  40.9 us (96%)
  local copies, waits for them, and re-layouts  1.71 us (4%)
    pallas_call x1, Pallas kernels, local_workers(): pl.pallas_call(functools.partial(cycle_kernel, groups, members), out_shap...  40.9 us
    unnamed x1, local copies, waits for them, and re-layouts  1.71 us

profile of v6, /device:TPU:0, one launch (start us, length us, event | category | flops | bytes accessed | tf_op | source)
XLA Modules:
  0.0 42.6 jit_solution(10549773813249829201)
XLA Ops:
  0.0 40.9 %shard_map.55 = bf16[1,1,384,384]{3,2,1,0:T(8,128)(2,1)} custom-call(bf16[1,1,384,384]{3,2,1,0:T(8,128)(2,1)} %amp_hbm.1, bf16[1,1,384,384]{3,2,1,0:T(8,128)(2,1)} %integ.1, s32[3,1,512]{2,1,0:T(1,128)} %bitcast.1, s32[1,8]{1,0:T(1,128)} %counts_hbm.1, s32[8]{0:T(128)} %owner_hbm.1), custom_call_target="tpu_custom_call" | custom-call | tf_op jit(solution)/shard_map/pallas_call | solution.py:334
  40.9 1.7 %copy.7 = bf16[1,1,384,384]{3,2,1,0:T(8,128)(2,1)} copy(bf16[1,1,384,384]{3,2,1,0:T(8,128)(2,1)} %shard_map.55) | data formatting | bytes 589824

commit v7 on v5

--- a/solution.py
+++ b/solution.py
@@ -112,8 +112,8 @@
     groups, members,
     amp_hbm, integ, tasks_hbm, counts_hbm, owner_hbm, out,
     amp, tasks, counts, owner,
-    swap, halves, mixed_t, got_t, weighed, given, taken, kept, final, spread,
-    swap_ss, swap_rs, int_ss, int_rs, mix_ss, mix_rs, part_ss, part_rs, out_ss, out_rs, local_sem,
+    swap, halves, mixed_t, got_t, weighed, given, taken, kept, final, landed, passing, spread,
+    swap_ss, swap_rs, int_ss, int_rs, mix_ss, mix_rs, part_ss, part_rs, out_ss, out_rs, pass_ss, pass_rs, local_sem,
 ):
     grp, mem = lax.axis_index("grp"), lax.axis_index("mem")
     tile = amp.shape[-1]
@@ -122,6 +122,8 @@
     partner = mem + 1 - 2 * side
     work_plane = planes // 2 - 1 + lax.rem(grp, 2)
     works = plane == work_plane
+    outer_plane = lax.rem(grp, 2) * (planes - 1)
+    adds = plane == outer_plane
     own_rows = pl.ds(pl.multiple_of(side * half, half), half)
 
     amp_in = pltpu.make_async_copy(amp_hbm, amp, local_sem.at[0])
@@ -158,7 +160,8 @@
             pl.semaphore_signal(
                 barrier, inc=1, device_id={"mem": work_plane * 2 + worker_side}, device_id_type=MESH
             )
-        pl.semaphore_wait(barrier, groups + 1)
+        pl.semaphore_signal(barrier, inc=1, device_id={"mem": partner}, device_id_type=MESH)
+        pl.semaphore_wait(barrier, groups + 2)
 
     def swap_copy(peer):
         return remote(
@@ -186,6 +189,20 @@
             part_ss.at[turn, row], part_rs.at[turn, row], mem=partner,
         )
 
+    def outer_copy(turn, kind):
+        return remote(
+            final.at[turn, outer_plane] if kind == 0 else given.at[turn, outer_plane],
+            landed.at[turn, side] if kind == 0 else passing.at[turn],
+            pass_ss.at[turn, kind], pass_rs.at[turn, side if kind == 0 else 2],
+            mem=outer_plane * 2 + side,
+        )
+
+    def pass_copy(turn):
+        return remote(
+            passing.at[turn], landed.at[turn, side],
+            pass_ss.at[turn, 0], pass_rs.at[turn, side], mem=partner,
+        )
+
     def out_copy(turn, row):
         return remote(
             final.at[turn, row], out.at[0, 0, pl.ds(turn * STEP, STEP)],
@@ -194,7 +211,7 @@
 
     def own_copy(turn):
         return pltpu.make_async_copy(
-            final.at[turn, plane], out.at[0, 0, pl.ds(turn * STEP, STEP)], out_rs.at[turn]
+            final.at[turn, plane], out.at[0, 0, pl.ds(turn * STEP, STEP)], out_rs.at[turn],
         )
 
     def to_workers(do):
@@ -257,12 +274,14 @@
 
         def finish(turn):
             for row in range(planes):
-                part_copy(turn, row).wait_recv()
-                final[turn, row] = (
-                    kept[turn, row] + taken[turn, row].astype(jnp.float32)
-                ).astype(jnp.bfloat16)
-
-                @pl.when(plane != row)
+                @pl.when(outer_plane != row)
+                def _():
+                    part_copy(turn, row).wait_recv()
+                    final[turn, row] = (
+                        kept[turn, row] + taken[turn, row].astype(jnp.float32)
+                    ).astype(jnp.bfloat16)
+
+                @pl.when((outer_plane != row) & (plane != row))
                 def _():
                     out_copy(turn, row).start()
 
@@ -286,27 +305,65 @@
                     preferred_element_type=jnp.float32,
                 )
 
+            given[turn, outer_plane] = multiply(outer_plane * 2 + 1 - side).astype(jnp.bfloat16)
+            outer_copy(turn, 1).start()
             for row in range(planes):
-                given[turn, row] = multiply(row * 2 + 1 - side).astype(jnp.bfloat16)
-                part_copy(turn, row).start()
+                @pl.when(outer_plane != row)
+                def _():
+                    given[turn, row] = multiply(row * 2 + 1 - side).astype(jnp.bfloat16)
+                    part_copy(turn, row).start()
+            final[turn, outer_plane] = multiply(outer_plane * 2 + side).astype(jnp.bfloat16)
+            outer_copy(turn, 0).start()
             for row in range(planes):
-                kept[turn, row] = multiply(row * 2 + side)
+                @pl.when(outer_plane != row)
+                def _():
+                    kept[turn, row] = multiply(row * 2 + side)
             if turn:
                 finish(turn - 1)
         finish(rounds - 1)
         for turn in range(rounds):
             own_copy(turn).wait()
+            for kind in range(2):
+                outer_copy(turn, kind).wait_send()
             for row in range(planes):
-                part_copy(turn, row).wait_send()
-
-                @pl.when(plane != row)
+                @pl.when(outer_plane != row)
+                def _():
+                    part_copy(turn, row).wait_send()
+
+                @pl.when((outer_plane != row) & (plane != row))
                 def _():
                     out_copy(turn, row).wait_send()
 
-    @pl.when(jnp.logical_not(works))
+    @pl.when(jnp.logical_not(works | adds))
     def _():
         for turn in range(rounds):
             out_copy(turn, 0).wait_recv()
+
+    @pl.when(adds)
+    def _():
+        def pass_arrival(turn, kind):
+            target = passing.at[turn] if kind == 2 else landed.at[turn, kind]
+            return remote(
+                target, target, pass_ss.at[turn, 0], pass_rs.at[turn, kind], mem=partner
+            )
+
+        def add(turn):
+            for worker_side in range(2):
+                pass_arrival(turn, worker_side).wait_recv()
+            final[turn, plane] = (
+                landed[turn, 0].astype(jnp.float32) + landed[turn, 1].astype(jnp.float32)
+            ).astype(jnp.bfloat16)
+            own_copy(turn).start()
+
+        for turn in range(rounds):
+            pass_arrival(turn, 2).wait_recv()
+            pass_copy(turn).start()
+            if turn:
+                add(turn - 1)
+        add(rounds - 1)
+        for turn in range(rounds):
+            pass_copy(turn).wait_send()
+            own_copy(turn).wait()
 
     for turn in range(1, groups):
         swap_copy(lax.rem(grp + turn, groups)).wait_send()
@@ -341,12 +398,15 @@
             pltpu.VMEM((rounds, planes, STEP, tile), bf16),
             pltpu.VMEM((rounds, planes, STEP, tile), jnp.float32),
             pltpu.VMEM((rounds, planes, STEP, tile), bf16),
+            pltpu.VMEM((rounds, 2, STEP, tile), bf16),
+            pltpu.VMEM((rounds, STEP, tile), bf16),
             pltpu.VMEM((members * members * BAND, members * BAND), bf16),
             dma((groups,)), dma((groups,)),
             dma((2,)), dma((members,)),
             dma((rounds, 2)), dma((rounds, members)),
             dma((rounds, planes)), dma((rounds, planes)),
             dma((rounds, planes)), dma((rounds,)),
+            dma((rounds, 2)), dma((rounds, 3)),
             dma((5,)),
         ],
         compiler_params=pltpu.CompilerParams(

time: 38.5 us -> 36.9 us (0.958); the launches traced: 37.9 us -> 36.8 us
  Pallas kernels: 36.2 us -> 35 us
    pallas_call x1, Pallas kernels: 36.2 us -> 35 us  [local_workers(): pl.pallas_call(functools.partial(cycle_kernel, groups, members), out_shap...]
where the time goes in v7:
time: 36.9 us; the launch traced here: 36.8 us
  Pallas kernels  35 us (95%)
  local copies, waits for them, and re-layouts  1.71 us (5%)
    pallas_call x1, Pallas kernels, local_workers(): pl.pallas_call(functools.partial(cycle_kernel, groups, members), out_shap...  35 us
    unnamed x1, local copies, waits for them, and re-layouts  1.71 us

profile of v7, /device:TPU:0, one launch (start us, length us, event | category | flops | bytes accessed | tf_op | source)
XLA Modules:
  0.0 36.8 jit_solution(15984887585854490061)
XLA Ops:
  0.0 35.0 %shard_map.55 = bf16[1,1,384,384]{3,2,1,0:T(8,128)(2,1)} custom-call(bf16[1,1,384,384]{3,2,1,0:T(8,128)(2,1)} %amp_hbm.1, bf16[1,1,384,384]{3,2,1,0:T(8,128)(2,1)} %integ.1, s32[3,1,512]{2,1,0:T(1,128)} %bitcast.1, s32[1,8]{1,0:T(1,128)} %counts_hbm.1, s32[8]{0:T(128)} %owner_hbm.1), custom_call_target="tpu_custom_call" | custom-call | tf_op jit(solution)/shard_map/pallas_call | solution.py:382
  35.0 1.7 %copy.7 = bf16[1,1,384,384]{3,2,1,0:T(8,128)(2,1)} copy(bf16[1,1,384,384]{3,2,1,0:T(8,128)(2,1)} %shard_map.55) | data formatting | bytes 589824

commit v8 on v7

--- a/solution.py
+++ b/solution.py
@@ -68,6 +68,7 @@
 MESH = pl.DeviceIdType.MESH
 STEP = 128
 BAND = 32
+PIECE = 2 * BAND
 VMEM_BYTES = 65280 * 1024
 
 
@@ -118,6 +119,7 @@
     grp, mem = lax.axis_index("grp"), lax.axis_index("mem")
     tile = amp.shape[-1]
     half, block, rounds, planes = tile // 2, tile // groups, tile // STEP, members // 2
+    pieces = half // PIECE
     plane, side = lax.div(mem, 2), lax.rem(mem, 2)
     partner = mem + 1 - 2 * side
     work_plane = planes // 2 - 1 + lax.rem(grp, 2)
@@ -169,10 +171,11 @@
             swap.at[grp], swap_ss.at[peer], swap_rs.at[grp], grp=peer,
         )
 
-    def int_copy(worker_side):
-        return remote(
-            integ.at[0, 0, pl.ds(worker_side * half, half)],
-            halves.at[mem], int_ss.at[worker_side], int_rs.at[mem],
+    def int_copy(piece, worker_side):
+        return remote(
+            integ.at[0, 0, pl.ds(worker_side * half + piece * PIECE, PIECE)],
+            halves.at[mem, pl.ds(piece * PIECE, PIECE)],
+            int_ss.at[piece, worker_side], int_rs.at[piece, mem],
             mem=work_plane * 2 + worker_side,
         )
 
@@ -222,7 +225,8 @@
 
     for turn in range(1, groups):
         swap_copy(lax.rem(grp + turn, groups)).start()
-    to_workers(lambda worker_side: int_copy(worker_side).start())
+    for piece in range(pieces):
+        to_workers(lambda worker_side: int_copy(piece, worker_side).start())
 
     amp_in.wait()
     own_block = pl.ds(pl.multiple_of(grp * block, block), block)
@@ -253,24 +257,29 @@
         owner_in.wait()
         half_in.wait()
         spread[...] = spread_counts(members, tasks, counts, owner)
-        for source in range(members):
-            @pl.when(mem != source)
-            def _():
-                remote(
-                    halves.at[source], halves.at[source],
-                    int_ss.at[0], int_rs.at[source], mem=partner,
-                ).wait_recv()
-
-        def weigh(index, carry):
-            rows = pl.ds(pl.multiple_of(index * BAND, BAND), BAND)
+        for piece in range(pieces):
+            first = piece * PIECE
+            for source in range(members):
+                @pl.when(mem != source)
+                def _():
+                    arrived = halves.at[source, pl.ds(first, PIECE)]
+                    remote(
+                        arrived, arrived, int_ss.at[0, 0], int_rs.at[piece, source], mem=partner
+                    ).wait_recv()
+            bands = [
+                halves[:, pl.ds(first + band * BAND, BAND)].reshape(members * BAND, tile)
+                for band in range(2)
+            ]
             sums = jnp.dot(
-                spread[...], halves[:, rows].reshape(members * BAND, tile),
-                preferred_element_type=jnp.float32,
-            )
-            weighed[:, :, rows] = sums.astype(jnp.bfloat16).reshape(members, members, BAND, tile)
-            return carry
-
-        lax.fori_loop(0, half // BAND, weigh, 0)
+                spread[...], jnp.concatenate(bands, axis=1), preferred_element_type=jnp.float32
+            ).astype(jnp.bfloat16)
+            for band in range(2):
+                rows = pl.ds(first + band * BAND, BAND)
+                for target in range(members):
+                    high = members * BAND
+                    weighed[target % 2, :, rows, pl.ds(target // 2 * tile, tile)] = sums[
+                        target * high : (target + 1) * high, band * tile : (band + 1) * tile
+                    ].reshape(members, BAND, tile)
 
         def finish(turn):
             for row in range(planes):
@@ -299,25 +308,34 @@
                     ).wait_recv()
             left = got_t[turn].reshape(members * half, STEP).T
 
-            def multiply(target):
-                return jnp.dot(
-                    left, weighed[target].reshape(members * half, tile),
-                    preferred_element_type=jnp.float32,
+            def multiply(target_side, pair):
+                wide = 2 * tile
+                right = weighed[target_side, :, :, pl.ds(pair * wide, wide)]
+                both = jnp.dot(
+                    left, right.reshape(members * half, wide), preferred_element_type=jnp.float32
                 )
-
-            given[turn, outer_plane] = multiply(outer_plane * 2 + 1 - side).astype(jnp.bfloat16)
-            outer_copy(turn, 1).start()
-            for row in range(planes):
-                @pl.when(outer_plane != row)
-                def _():
-                    given[turn, row] = multiply(row * 2 + 1 - side).astype(jnp.bfloat16)
-                    part_copy(turn, row).start()
-            final[turn, outer_plane] = multiply(outer_plane * 2 + side).astype(jnp.bfloat16)
-            outer_copy(turn, 0).start()
-            for row in range(planes):
-                @pl.when(outer_plane != row)
-                def _():
-                    kept[turn, row] = multiply(row * 2 + side)
+                return [(pair * 2, both[:, :tile]), (pair * 2 + 1, both[:, tile:])]
+
+            for pair in range(planes // 2):
+                for row, product in multiply(1 - side, pair):
+                    given[turn, row] = product.astype(jnp.bfloat16)
+
+                    @pl.when(outer_plane == row)
+                    def _():
+                        outer_copy(turn, 1).start()
+
+                    @pl.when(outer_plane != row)
+                    def _():
+                        part_copy(turn, row).start()
+            for pair in range(planes // 2):
+                for row, product in multiply(side, pair):
+                    kept[turn, row] = product
+
+                    @pl.when(outer_plane == row)
+                    def _():
+                        final[turn, row] = kept[turn, row].astype(jnp.bfloat16)
+                        outer_copy(turn, 0).start()
+
             if turn:
                 finish(turn - 1)
         finish(rounds - 1)
@@ -367,7 +385,8 @@
 
     for turn in range(1, groups):
         swap_copy(lax.rem(grp + turn, groups)).wait_send()
-    to_workers(lambda worker_side: int_copy(worker_side).wait_send())
+    for piece in range(pieces):
+        to_workers(lambda worker_side: int_copy(piece, worker_side).wait_send())
     for turn in range(rounds):
         to_workers(lambda worker_side: mix_copy(turn, worker_side).wait_send())
 
@@ -393,7 +412,7 @@
             pltpu.VMEM((members, half, tile), bf16),
             pltpu.VMEM((rounds, tile, STEP), bf16),
             pltpu.VMEM((rounds, members, half, STEP), bf16),
-            pltpu.VMEM((members, members, half, tile), bf16),
+            pltpu.VMEM((2, members, half, planes * tile), bf16),
             pltpu.VMEM((rounds, planes, STEP, tile), bf16),
             pltpu.VMEM((rounds, planes, STEP, tile), bf16),
             pltpu.VMEM((rounds, planes, STEP, tile), jnp.float32),
@@ -402,7 +421,7 @@
             pltpu.VMEM((rounds, STEP, tile), bf16),
             pltpu.VMEM((members * members * BAND, members * BAND), bf16),
             dma((groups,)), dma((groups,)),
-            dma((2,)), dma((members,)),
+            dma((half // PIECE, 2)), dma((half // PIECE, members)),
             dma((rounds, 2)), dma((rounds, members)),
             dma((rounds, planes)), dma((rounds, planes)),
             dma((rounds, planes)), dma((rounds,)),

time: 36.9 us -> 35 us (0.949)
  Pallas kernels: 35 us -> 33.1 us
    pallas_call x1, Pallas kernels: 35 us -> 33.1 us  [local_workers(): pl.pallas_call(functools.partial(cycle_kernel, groups, members), out_shap...]
where the time goes in v8:
time: 35 us; the launch traced here: 34.8 us
  Pallas kernels  33.1 us (95%)
  local copies, waits for them, and re-layouts  1.71 us (5%)
    pallas_call x1, Pallas kernels, local_workers(): pl.pallas_call(functools.partial(cycle_kernel, groups, members), out_shap...  33.1 us
    unnamed x1, local copies, waits for them, and re-layouts  1.71 us

profile of v8, /device:TPU:0, one launch (start us, length us, event | category | flops | bytes accessed | tf_op | source)
XLA Modules:
  0.0 34.8 jit_solution(17788265841380424427)
XLA Ops:
  0.0 33.1 %shard_map.55 = bf16[1,1,384,384]{3,2,1,0:T(8,128)(2,1)} custom-call(bf16[1,1,384,384]{3,2,1,0:T(8,128)(2,1)} %amp_hbm.1, bf16[1,1,384,384]{3,2,1,0:T(8,128)(2,1)} %integ.1, s32[3,1,512]{2,1,0:T(1,128)} %bitcast.1, s32[1,8]{1,0:T(1,128)} %counts_hbm.1, s32[8]{0:T(128)} %owner_hbm.1), custom_call_target="tpu_custom_call" | custom-call | tf_op jit(solution)/shard_map/pallas_call | solution.py:401
  33.1 1.7 %copy.7 = bf16[1,1,384,384]{3,2,1,0:T(8,128)(2,1)} copy(bf16[1,1,384,384]{3,2,1,0:T(8,128)(2,1)} %shard_map.55) | data formatting | bytes 589824
